TPU v7x, 256 devices: a whole 4x4x8 slice. The times are simulated.
256 devices in a mesh: dp: 8 (over z), db: 32 (over y, x, core).
Axes of the slice: x: 4, y: 4, z: 8, core: 2. Of those that a mesh axis runs over, the one named last changes fastest.
Arguments:
- queries: bfloat16 [65536, 2048], P(('dp', 'db')), may hold values from -90 to 90
- grad_out: bfloat16 [65536, 2048], P(('dp', 'db')), may hold values from -6 to 6
- neighbour_ids: int32 [1024, 2], P(('dp', 'db')), may hold values from 0 to 255, as said below
- entry_home: int32 [256], replicated, may hold values from 0 to 255, as said below
- cache: bfloat16 [256, 128, 512], P('db'), may hold values from -6 to 6
- kv_weight: bfloat16 [512, 4096], replicated, may hold values from -0.25 to 0.25
Outputs:
- attended: bfloat16 [65536, 2048], P(('dp', 'db'))
- query_grad: bfloat16 [65536, 2048], P(('dp', 'db'))
- weight_grad: float32 [512, 4096], P(('dp', 'db'))
Inputs may be any that keep to these rules, and one draw needn't show every extreme that they name: `neighbour_ids`: over the 4 stretches of one device at most 1 neighbours are stored on one shard (shard = entry_home[id] // 8), and some shard holds exactly 1 of them; the 2 neighbours of a stretch are stored on different shards. `entry_home`: A permutation: every position is taken once.
All inputs are finite; a program needn't handle non-finite values.
Results may differ from a plain program's by a relative error of at most 0.012.
The roundings to bfloat16 on the way count: a program that leaves them out, or rounds other values in their place, can miss the bound.
Values may be sent and summed in bfloat16 or wider, within the bound.
No kernel may reach another device: no remote copies, remote signals or barrier semaphores. Data moves between devices by JAX's collectives and lax.ppermute only.
A program may use at most 128 MiB of HBM per device.

v0:
```python
import jax
import jax.numpy as jnp
from jax import lax
from jax.sharding import PartitionSpec as P

DH = 128
STRETCH = 64
CAP = 1


def attention_pass(queries, grad_out, fetched, kv_weight):
    width = queries.shape[1]
    heads = width // DH
    nchunk = queries.shape[0] // STRETCH
    keys_len = fetched.shape[0] // nchunk
    projected = jnp.dot(fetched, kv_weight, preferred_element_type=jnp.float32).astype(jnp.bfloat16)
    keys = projected[:, :width].reshape(nchunk, keys_len, heads, DH)
    values = projected[:, width:].reshape(nchunk, keys_len, heads, DH)
    query_h = queries.reshape(nchunk, STRETCH, heads, DH)
    grad_h = grad_out.reshape(nchunk, STRETCH, heads, DH)
    scale = DH ** (-0.5)
    scores = (
        jnp.einsum("cqhd,ckhd->chqk", query_h, keys, preferred_element_type=jnp.float32) * scale
    )
    top = jnp.max(scores, axis=-1, keepdims=True)
    expo = jnp.exp(scores - top)
    probs = expo / jnp.sum(expo, axis=-1, keepdims=True)
    probs_b = probs.astype(jnp.bfloat16)
    context = jnp.einsum("chqk,ckhd->cqhd", probs_b, values, preferred_element_type=jnp.float32)
    delta = jnp.sum(grad_h.astype(jnp.float32) * context, axis=-1)
    dprob = jnp.einsum("cqhd,ckhd->chqk", grad_h, values, preferred_element_type=jnp.float32)
    dscore = (probs * (dprob - jnp.transpose(delta, (0, 2, 1))[..., None])).astype(jnp.bfloat16)
    query_grad = (
        jnp.einsum("chqk,ckhd->cqhd", dscore, keys, preferred_element_type=jnp.float32) * scale
    ).astype(jnp.bfloat16)
    key_grad = (
        jnp.einsum("chqk,cqhd->ckhd", dscore, query_h, preferred_element_type=jnp.float32) * scale
    )
    value_grad = jnp.einsum("chqk,cqhd->ckhd", probs_b, grad_h, preferred_element_type=jnp.float32)
    kv_grad = jnp.concatenate(
        [key_grad.reshape(-1, width), value_grad.reshape(-1, width)], axis=1
    ).astype(jnp.bfloat16)
    attended = context.astype(jnp.bfloat16).reshape(-1, width)
    return (attended, query_grad.reshape(-1, width), kv_grad)


def body(queries, grad_out, neighbour_ids, entry_home, cache, kv_weight):
    n_db = lax.axis_size("db")
    ent_dev = cache.shape[0]
    rows_each = cache.shape[1]
    features = cache.shape[2]
    wanted = neighbour_ids.reshape(-1)
    count = wanted.shape[0]
    entries = entry_home.shape[0]
    match = wanted[:, None] == jnp.arange(entries, dtype=jnp.int32)[None, :]
    position = jnp.sum(jnp.where(match, entry_home[None, :], 0), axis=1)
    shard = position // ent_dev
    local = position % ent_dev
    earlier = (
        jnp.arange(count, dtype=jnp.int32)[:, None] > jnp.arange(count, dtype=jnp.int32)[None, :]
    )
    same = shard[:, None] == shard[None, :]
    slot = jnp.sum(jnp.where(earlier & same, 1, 0), axis=1).astype(jnp.int32)
    place = shard * CAP + slot
    target = place[:, None] == jnp.arange(n_db * CAP, dtype=jnp.int32)[None, :]
    request = jnp.sum(jnp.where(target, local[:, None], 0), axis=0).reshape(n_db, CAP)
    asked = lax.all_to_all(request, "db", split_axis=0, concat_axis=0, tiled=True)
    served = cache[asked.reshape(-1)].reshape(n_db, CAP, rows_each, features)
    answer = lax.all_to_all(served, "db", split_axis=0, concat_axis=0, tiled=True)
    fetched = answer.reshape(n_db * CAP, rows_each, features)[place].reshape(
        count * rows_each, features
    )
    attended, query_grad, kv_grad = attention_pass(queries, grad_out, fetched, kv_weight)
    weight_grad = lax.psum_scatter(
        lax.dot_general(
            fetched, kv_grad, (((0,), (0,)), ((), ())), preferred_element_type=jnp.float32
        ),
        ("dp", "db"),
        scatter_dimension=0,
        tiled=True,
    )
    return (attended, query_grad, weight_grad)


def solution(mesh):
    return jax.shard_map(
        body,
        mesh=mesh,
        in_specs=(
            P(("dp", "db"), None),
            P(("dp", "db"), None),
            P(("dp", "db"), None),
            P(),
            P("db", None, None),
            P(),
        ),
        out_specs=(P(("dp", "db"), None), P(("dp", "db"), None), P(("dp", "db"), None)),
        check_vma=False,
    )
```

profile of v0, /device:TPU:1, one launch (start us, length us, event | category | flops | bytes accessed | tf_op | source)
XLA Modules:
  0.0 444.1 jit_solution(14705731866635123465)
XLA Ops:
  7.2 0.0 copy-start
  7.2 0.9 copy.60
  8.0 0.1 eq.22
  8.1 0.9 select_reduce_fusion
  9.0 0.2 select_reduce_fusion.2
  9.2 0.1 select_reduce_fusion.1
  9.3 0.1 copy.61
  9.4 15.3 %all_to_all.17 = s32[32,1,1]{2,1,0:T(1,128)S(1)} all-to-all(s32[32,1,1]{2,1,0:T(1,128)S(1)} %copy.61), channel_id=1, replica_groups=mesh['dp'=8,'db'=32] {'db'}, dimensions={0} | all-to-all | bytes 256 | tf_op jit(solution)/shard_map/all_to_all | solution.py:67
  24.7 0.7 reduce
  25.4 0.0 copy-done
  25.4 2.8 gather_fusion
  28.2 5.2 %all-to-all-start.1 = ((bf16[32,1,128,512]{3,2,1,0:T(8,128)(2,1)}), bf16[32,1,128,512]{3,2,1,0:T(8,128)(2,1)}, u32[]{:S(2)}, u32[]{:S(2)}) async-start(bf16[32,1,128,512]{3,2,1,0:T(8,128)(2,1)} %bitcast.108), calls=%async_computation.1 | async-start | bytes 8388608 | tf_op jit(solution)/shard_map/all_to_all | solution.py:69
  33.4 0.0 all-reduce.3.cloned.1.call-start
  33.4 0.0 copy-done.8
  33.4 0.2 copy.76
  33.7 0.0 copy-done.9
  33.7 0.2 copy.79
  34.0 49.8 %all-to-all-done.1 = bf16[32,1,128,512]{3,2,1,0:T(8,128)(2,1)} async-done(((bf16[32,1,128,512]{3,2,1,0:T(8,128)(2,1)}), bf16[32,1,128,512]{3,2,1,0:T(8,128)(2,1)}, u32[]{:S(2)}, u32[]{:S(2)}) %all-to-all-start.1) | async-done | bytes 4194336 | tf_op jit(solution)/shard_map/all_to_all | solution.py:69
  83.8 2.8 gather_fusion.1
  86.6 6.9 %convolution_convert_fusion = bf16[1024,4096]{1,0:T(8,128)(2,1)S(1)} fusion(bf16[1024,512]{1,0:T(8,128)(2,1)S(1)} %bitcast.120, bf16[512,4096]{1,0:T(8,128)(2,1)} %param.11), kind=kOutput, calls=%fused_computation.8 | convolution fusion | flops 4299161600 | bytes 13631488 | tf_op jit(solution)/shard_map/dot_general | solution.py:16
  93.5 1.2 slice_bitcast_fusion.1
  94.7 3.3 copy.77
  98.0 1.4 copy.75
  99.5 0.0 copy-start.2
  99.5 1.6 fusion.15
  101.1 0.3 copy-done.2
  101.4 3.3 fusion.49
  104.7 0.0 copy-done.3
  104.7 13.6 %bitcast_convert_fusion = (bf16[4,64,16,128]{3,1,2,0:T(8,128)(2,1)}, f32[4,16,128,64]{2,3,1,0:T(8,128)}) fusion(bf16[4,256,16,128]{3,2,1,0:T(8,128)(2,1)} %bitcast.116, f32[4,16,64]{2,1,0:T(8,128)S(1)} %get-tuple-element.7, f32[4,16,256,64]{2,3,1,0:T(8,128)} %copy-done.3), kind=kOutput, calls=%fused_computation.31 | convolution fusion | flops 274206976 | bytes 11550720 | tf_op jit(solution)/shard_map/chqk,ckhd->cqhd/dot_general | solution.py:29
  118.2 13.5 %convert_bitcast_fusion = bf16[4,256,16,128]{3,1,2,0:T(8,128)(2,1)} fusion(bf16[4,64,16,128]{3,2,1,0:T(8,128)(2,1)S(1)} %bitcast.113, f32[4,16,64]{2,1,0:T(8,128)S(1)} %get-tuple-element.7, f32[4,16,256,64]{2,3,1,0:T(8,128)} %copy-done.3), kind=kOutput, calls=%fused_computation.20 | convolution fusion | flops 275779840 | bytes 9453568 | tf_op jit(solution)/shard_map/chqk,cqhd->ckhd/dot_general | solution.py:39
  131.7 2.2 fusion.20
  134.0 0.0 copy-start.4
  134.0 0.0 copy-start.5
  134.0 5.0 %copy.74 = bf16[4,256,16,128]{3,2,1,0:T(8,128)(2,1)S(1)} copy(bf16[4,256,16,128]{3,1,2,0:T(8,128)(2,1)} %convert_bitcast_fusion) | data formatting | bytes 8388608 | tf_op jit(solution)/shard_map/chqk,cqhd->ckhd/transpose | solution.py:39
  139.0 2.2 fusion.6
  141.3 1.6 fusion.5
  142.9 2.7 copy.72
  145.6 4.7 %copy_bitcast_fusion = (bf16[1024,2048]{1,0:T(8,128)(2,1)S(1)}, bf16[1024,2048]{1,0:T(8,128)(2,1)S(1)}) fusion(bf16[128,8,16,128]{3,2,1,0:T(8,128)(2,1)S(1)} %bitcast.109, bf16[128,8,16,128]{3,2,1,0:T(8,128)(2,1)S(1)} %bitcast.110), kind=kLoop, calls=%fused_computation.10 | loop fusion | bytes 16777216 | tf_op jit(solution)/shard_map/reshape | solution.py:41
  150.3 6.9 %fusion.1 = f32[512,4096]{1,0:T(8,128)} fusion(bf16[1024,512]{1,0:T(8,128)(2,1)S(1)} %bitcast.121, bf16[1024,2048]{1,0:T(8,128)(2,1)S(1)} %get-tuple-element.11, bf16[1024,2048]{1,0:T(8,128)(2,1)S(1)} %get-tuple-element.12), kind=kOutput, calls=%fused_computation.3 | convolution fusion | flops 4311744512 | bytes 17825792 | tf_op jit(solution)/shard_map/dot_general | solution.py:75
  157.2 0.0 all-reduce.3.cloned.1.call-update
  157.3 1.6 copy-done.7
  158.8 3.7 fusion.27
  162.5 0.7 copy.70
  163.2 0.7 copy.65
  163.9 1.8 copy_bitcast_fusion.2
  165.7 270.0 %all-reduce.3.cloned.1.call-done = f32[512,4096]{1,0:T(8,128)} async-done(((f32[512,4096]{1,0:T(8,128)}), f32[512,4096]{1,0:T(8,128)}) %all-reduce.3.cloned.1.call-update) | async-done | bytes 8388624
  435.8 1.5 constant_dynamic-slice_fusion
  437.3 0.0 copy-done.1
  (17 shorter events, 0.1 us)
Async XLA Ops:
  7.2 18.2 %copy-start = (bf16[8,128,512]{2,1,0:T(8,128)(2,1)S(1)}, bf16[8,128,512]{2,1,0:T(8,128)(2,1)}, u32[]{:S(2)}) copy-start(bf16[8,128,512]{2,1,0:T(8,128)(2,1)} %param.10) | copy-start | bytes 3145732
  28.2 5.3 %copy-start.8 = (bf16[256,2048]{1,0:T(8,128)(2,1)S(1)}, bf16[256,2048]{1,0:T(8,128)(2,1)}, u32[]{:S(2)}) copy-start(bf16[256,2048]{1,0:T(8,128)(2,1)} %param.6) | copy-start | bytes 3145732
  28.2 5.5 %copy-start.9 = (bf16[256,2048]{1,0:T(8,128)(2,1)S(1)}, bf16[256,2048]{1,0:T(8,128)(2,1)}, u32[]{:S(2)}) copy-start(bf16[256,2048]{1,0:T(8,128)(2,1)} %param.7) | copy-start | bytes 3145732
  28.2 55.6 %all-to-all-start.1 = ((bf16[32,1,128,512]{3,2,1,0:T(8,128)(2,1)}), bf16[32,1,128,512]{3,2,1,0:T(8,128)(2,1)}, u32[]{:S(2)}, u32[]{:S(2)}) async-start(bf16[32,1,128,512]{3,2,1,0:T(8,128)(2,1)} %bitcast.108), calls=%async_computation.1 | async-start | bytes 8388608 | tf_op jit(solution)/shard_map/all_to_all | solution.py:69
  33.4 402.4 %all-reduce.3.cloned.1.call-start = ((), (), s32[]{:S(2)}) async-start(), calls=%async_computation.2 | async-start | bytes 16777216
  99.5 1.9 copy-start.2
  101.4 3.3 copy-start.3
  134.0 5.1 %copy-start.4 = (bf16[128,8,16,128]{3,2,1,0:T(8,128)(2,1)S(1)}, bf16[128,8,16,128]{3,2,1,0:T(8,128)(2,1)}, u32[]{:S(2)}) copy-start(bf16[128,8,16,128]{3,2,1,0:T(8,128)(2,1)} %copy.77) | copy-start | bytes 12582916
  134.0 5.1 %copy-start.5 = (f32[4,16,64,256]{3,2,1,0:T(8,128)S(1)}, f32[4,16,64,256]{3,2,1,0:T(8,128)}, u32[]{:S(2)}) copy-start(f32[4,16,64,256]{3,2,1,0:T(8,128)} %get-tuple-element.8) | copy-start | bytes 12582916
  141.3 4.3 copy-start.6
  157.2 1.6 copy-start.7
  158.8 4.4 copy-start.10
  158.8 278.5 %copy-start.1 = (bf16[8,128,512]{2,1,0:T(8,128)(2,1)S(1)}, bf16[8,128,512]{2,1,0:T(8,128)(2,1)}, u32[]{:S(2)}) copy-start(bf16[8,128,512]{2,1,0:T(8,128)(2,1)} %param.10) | copy-start | bytes 3145732
Sparse Core Ops, SparseCore 0:
  157.4 278.3 all-reduce.2
where the time goes:
time: 445 us; the launch traced here: 444 us
  waiting for transfers between devices  320 us (72%)
  matrix products  50 us (11%)
  local copies, waits for them, and re-layouts  32.1 us (7%)
  blocking collectives  15.3 us (3%)
  between operations  14.3 us (3%)
  other arithmetic  7.31 us (2%)
  starting transfers between devices  5.25 us (1%)
    unnamed x2, waiting for transfers between devices  270 us
    all_to_all x1, waiting for transfers between devices, body(): lax.all_to_all(served, 'db', split_axis=0, concat_axis=0, tiled=True)  49.8 us
    all_to_all x1, blocking collectives, body(): lax.all_to_all(request, 'db', split_axis=0, concat_axis=0, tiled=True)  15.3 us
    dot_general x1, matrix products, attention_pass(): jnp.einsum('chqk,ckhd->cqhd', probs_b, values, preferred_element_type=jnp...  13.6 us
    dot_general x1, matrix products, attention_pass(): jnp.einsum('chqk,cqhd->ckhd', probs_b, grad_h, preferred_element_type=jnp...  13.5 us
    unnamed x29, local copies, waits for them, and re-layouts  10.7 us
  transfers between devices with their start and end apart: 2, of which 2 were waited for; matrix products, arithmetic and copies ran while one was open for 2% of the time, Pallas kernels for 0%

commit v1 on v0

v1 whole, which is shorter than its diff:
```python
import functools

import jax
import jax.numpy as jnp
from jax import lax
from jax.experimental import pallas as pl
from jax.experimental.pallas import tpu as pltpu
from jax.sharding import Mesh, PartitionSpec as P

DH = 128
STRETCH = 64
NZ, NY, NX, NC = 8, 4, 4, 2
N_DB = NY * NX * NC
KEYS = 256
ROWS = 128
FEAT = 512
WANT = 8
PAIR = 2 * DH
STEPS = 32000.0
PARTS = 1
PAIRS = 2
WIDE = PAIRS * PAIR
RING = (0, 3, 1, 2)
TILE_R = 16
RB = ROWS // TILE_R
FB = FEAT // DH
NT = (((1,), (1,)), ((), ()))
TN = (((0,), (0,)), ((), ()))
ALL = ("z", "y", "x", "core")
PLANE = ("y", "x", "core")


def spread_kernel(coords_ref, ids_ref, home_ref, cache_ref, out_ref, sems):
    ents = cache_ref.shape[0]
    copies = []
    for rb in range(RB):
        for fb in range(FB):
            m = rb * FB + fb
            copies.append(
                pltpu.make_async_copy(
                    cache_ref.at[:, rb * TILE_R : (rb + 1) * TILE_R, fb * DH : (fb + 1) * DH],
                    out_ref.at[m, pl.ds(0, ents)],
                    sems.at[m],
                )
            )
    for cp in copies:
        cp.start()
    row = lax.broadcasted_iota(jnp.int32, (TILE_R, DH), 0)
    lane = lax.broadcasted_iota(jnp.int32, (TILE_R, DH), 1)
    tile = jnp.zeros((TILE_R, DH), jnp.float32)
    for k in range(WANT):
        spot = home_ref[ids_ref[k % 2, k // 2]].astype(jnp.float32)
        tile = jnp.where((row == 0) & (lane == k), spot, tile)
    tile = tile.astype(jnp.bfloat16)
    for m in range(RB * FB):
        out_ref[m, ents] = tile
    for cp in copies:
        cp.wait()


def pick_kernel(spots_ref, store_ref, out_ref):
    def one(d, carry):
        spots = [spots_ref[d, k] for k in range(WANT)]
        tiles = [store_ref[spot >> 3, spot & 7] for spot in spots]
        for k in range(WANT):
            out_ref[d * WANT + k] = tiles[k]
        return carry

    lax.fori_loop(0, out_ref.shape[0] // WANT, one, 0, unroll=8)


def encode(x):
    top = jnp.maximum(jnp.max(jnp.abs(x), axis=0, keepdims=True), 1e-36)
    power = jnp.ceil(jnp.log2(top))
    coded = jnp.round(x * jnp.exp2(-power) * STEPS).astype(jnp.int32)
    power = jnp.broadcast_to(power.astype(jnp.int32), (TILE_R, x.shape[1]))
    return coded.astype(jnp.int16), power.astype(jnp.int16)


def decode(ref):
    rows = ref.shape[0] - TILE_R
    power = ref[rows:, :].astype(jnp.int32)[:1].astype(jnp.float32)
    return ref[:rows, :].astype(jnp.int32).astype(jnp.float32) * (1.0 / STEPS) * jnp.exp2(power)


def put(ref, x):
    coded, power = encode(x)
    rows = ref.shape[0] - TILE_R
    ref[:rows, :] = coded
    ref[rows:, :] = power


def encode_rows(x):
    top = jnp.maximum(jnp.max(jnp.abs(x), axis=1, keepdims=True), 1e-36)
    power = jnp.ceil(jnp.log2(top))
    coded = jnp.round(x * jnp.exp2(-power) * STEPS).astype(jnp.int32)
    power = jnp.broadcast_to(power.astype(jnp.int32), (x.shape[0], DH))
    return coded.astype(jnp.int16), power.astype(jnp.int16)


def decode_rows(coded, power):
    power = power.astype(jnp.int32).astype(jnp.float32)[:, :1]
    return coded.astype(jnp.int32).astype(jnp.float32) * (1.0 / STEPS) * jnp.exp2(power)


def row_order(coords_ref):
    old = lax.broadcasted_iota(jnp.int32, (1, FEAT), 1)
    dx = ((old >> 2) & 3) ^ coords_ref[2]
    dy = ((old >> 4) & 3) ^ coords_ref[1]
    z = old >> 6
    px = jnp.where(dx == 3, 1, jnp.where(dx == 1, 2, jnp.where(dx == 2, 3, 0)))
    py = jnp.where(dy == 3, 1, jnp.where(dy == 1, 2, jnp.where(dy == 2, 3, 0)))
    core = coords_ref[3]
    first = jnp.where(core == 0, px, py)
    second = jnp.where(core == 0, py, px)
    place = first * 128 + second * 32 + z * 4 + (old & 3)
    new = lax.broadcasted_iota(jnp.int32, (FEAT, FEAT), 0)
    return jnp.where(new == place, 1.0, 0.0).astype(jnp.bfloat16)


def lay_rows(coords_ref, r_ref, rr_ref, f_ref, ft_ref, sems):
    copies = []
    for side, ref in enumerate((r_ref, rr_ref)):
        for rb in range(RB):
            for fb in range(FB):
                m = rb * FB + fb
                copies.append(
                    pltpu.make_async_copy(
                        ref.at[m],
                        f_ref.at[pl.ds(side * WANT, WANT), rb, :, fb * DH : (fb + 1) * DH],
                        sems.at[side * RB * FB + m],
                    )
                )
    copy_all(copies)
    f = f_ref[...].reshape(NC * WANT * ROWS, FEAT)
    ft_ref[...] = lax.dot_general(row_order(coords_ref), f, NT, preferred_element_type=jnp.float32).astype(
        jnp.bfloat16
    )


def first_kernel(coords_ref, r_ref, rr_ref, q_ref, g_ref, qg_ref, wk_ref, wv_ref, *refs):
    outs, f_ref, ft_ref, scratch, sems = refs[:6], refs[6], refs[7], refs[8:-1], refs[-1]

    @pl.when(pl.program_id(0) == 0)
    def _():
        lay_rows(coords_ref, r_ref, rr_ref, f_ref, ft_ref, sems)

    attend_kernel(coords_ref, f_ref, ft_ref, q_ref, g_ref, qg_ref, wk_ref, wv_ref, *outs, *scratch)


def attend_kernel(
    coords_ref, f_ref, ft_ref, q_ref, g_ref, qg_ref, wk_ref, wv_ref,
    own_ref, oth_ref, keepk_ref, sendk_ref, keepv_ref, sendv_ref,
    k_ref, v_ref, dk_ref, dv_ref,
):
    scale = DH ** (-0.5)
    tokens = q_ref.shape[0]
    every = NC * WANT * ROWS
    left = lax.broadcasted_iota(jnp.int32, (STRETCH, PAIR), 1) < DH
    zero = jnp.zeros((STRETCH, PAIR), jnp.bfloat16)
    f = f_ref[...].reshape(every, FEAT)

    def both(t):
        return jnp.concatenate([jnp.where(left, t, zero), jnp.where(left, zero, t)], axis=0)

    def query(s, cols):
        at = s * STRETCH
        ref, at = (q_ref, at) if at < tokens else (qg_ref, at - tokens)
        return both(ref[at : at + STRETCH, cols])

    def grad(s, cols):
        at = s * STRETCH
        ref = g_ref if at < tokens else qg_ref
        return both(ref[at : at + STRETCH, cols])

    def give(base, s, at_col, x):
        at = s * STRETCH
        ref, at = (own_ref, at) if at < tokens else (oth_ref, at - tokens)
        rows = slice(base + at, base + at + STRETCH)
        ref[rows, at_col : at_col + DH] = x[:STRETCH, :DH].astype(jnp.bfloat16)
        ref[rows, at_col + DH : at_col + PAIR] = x[STRETCH:, DH:].astype(jnp.bfloat16)

    items = [
        (s, slice(s * KEYS, (s + 1) * KEYS), slice(p * PAIR, (p + 1) * PAIR))
        for p in range(PAIRS)
        for s in range(NC * tokens // STRETCH)
    ]
    scores, dprob, pbs, ds = [], [], [], []
    k_ref[...] = jnp.dot(f, wk_ref[...], preferred_element_type=jnp.float32).astype(jnp.bfloat16)
    v_ref[...] = jnp.dot(f, wv_ref[...], preferred_element_type=jnp.float32).astype(jnp.bfloat16)
    for s, keys, cols in items:
        scores.append(
            lax.dot_general(k_ref[keys, cols], query(s, cols), NT, preferred_element_type=jnp.float32) * scale
        )
        dprob.append(lax.dot_general(v_ref[keys, cols], grad(s, cols), NT, preferred_element_type=jnp.float32))
    for x, dp in zip(scores, dprob):
        expo = jnp.exp(x - jnp.max(x, axis=0, keepdims=True))
        probs = expo * (1.0 / jnp.sum(expo, axis=0, keepdims=True))
        pb = probs.astype(jnp.bfloat16)
        delta = jnp.sum(pb.astype(jnp.float32) * dp, axis=0, keepdims=True)
        pbs.append(pb)
        ds.append((probs * (dp - delta)).astype(jnp.bfloat16))
    for i, (s, keys, cols) in enumerate(items):
        dv_ref[keys, cols] = jnp.dot(pbs[i], grad(s, cols), preferred_element_type=jnp.float32).astype(jnp.bfloat16)
        ctx = lax.dot_general(pbs[i], v_ref[keys, cols], TN, preferred_element_type=jnp.float32)
        give(0, s, cols.start, ctx)
    for i, (s, keys, cols) in enumerate(items):
        dk_ref[keys, cols] = (
            jnp.dot(ds[i], query(s, cols), preferred_element_type=jnp.float32) * scale
        ).astype(jnp.bfloat16)
        dq = lax.dot_general(ds[i], k_ref[keys, cols], TN, preferred_element_type=jnp.float32) * scale
        give(tokens, s, cols.start, dq)
    dwv = jnp.dot(ft_ref[...], dv_ref[...], preferred_element_type=jnp.float32)
    keepv_ref[:128, :] = dwv[:128]
    keepv_ref[128:, :] = dwv[256:384]
    put(sendv_ref, jnp.concatenate([dwv[128:256], dwv[384:]], axis=0))
    put(sendk_ref, jnp.dot(ft_ref[256:, :], dk_ref[...], preferred_element_type=jnp.float32))
    keepk_ref[...] = jnp.dot(ft_ref[:256, :], dk_ref[...], preferred_element_type=jnp.float32)


def attend(coords, rows, queries, grad_out, oth, kv_weight):
    tokens, width = queries.shape
    steps = width // WIDE // NC
    half = FEAT // 2
    every = NC * WANT * ROWS
    queries, grad_out, kv_weight = (
        pltpu.with_memory_space_constraint(a, pltpu.HBM) for a in (queries, grad_out, kv_weight)
    )
    mine = lambda rows, at0: pl.BlockSpec((rows, WIDE), lambda h, at: (0, at0 + at[3] * steps + h))
    col = lambda rows: pl.BlockSpec((rows, WIDE), lambda h, at: (0, h))
    shape = lambda rows, dtype: jax.ShapeDtypeStruct((rows, width // NC), dtype)
    return pl.pallas_call(
        first_kernel,
        grid_spec=pltpu.PrefetchScalarGridSpec(
            num_scalar_prefetch=1,
            grid=(steps,),
            in_specs=[pl.BlockSpec(memory_space=pl.ANY)] * 2
            + [mine(tokens, 0), mine(tokens, 0), col(2 * tokens), mine(FEAT, 0), mine(FEAT, NC * steps)],
            out_specs=[
                col(2 * tokens), col(2 * tokens),
                col(half), col(half + TILE_R), col(half), col(half + TILE_R),
            ],
            scratch_shapes=[
                pltpu.VMEM((NC * WANT, RB, TILE_R, FEAT), jnp.bfloat16),
                pltpu.VMEM((FEAT, every), jnp.bfloat16),
            ]
            + [pltpu.VMEM((every, WIDE), jnp.bfloat16)] * 4
            + [pltpu.SemaphoreType.DMA((NC * RB * FB,))],
        ),
        out_shape=[
            shape(2 * tokens, jnp.bfloat16), shape(2 * tokens, jnp.bfloat16),
            shape(half, jnp.float32), shape(half + TILE_R, jnp.int16),
            shape(half, jnp.float32), shape(half + TILE_R, jnp.int16),
        ],
        compiler_params=pltpu.CompilerParams(vmem_limit_bytes=36 * 2**20),
        cost_estimate=pl.CostEstimate(flops=11 * 10**9, bytes_accessed=8 * 2**20, transcendentals=10**6),
        name="attend",
    )(coords, *rows, queries, grad_out, oth, kv_weight, kv_weight)


def fold_kernel(kept_ref, came_ref, keep_ref, send_ref):
    rows = keep_ref.shape[0]
    total = kept_ref[...] + decode(came_ref)
    put(send_ref, total[rows:])
    keep_ref[...] = total[:rows]


def split_kernel(*refs):
    sums, keep_ref, send_refs = refs[: 4 * PARTS], refs[4 * PARTS], refs[4 * PARTS + 1 :]
    rows, width = keep_ref.shape
    wide = width // (2 * PARTS)
    for i in range(2 * PARTS):
        cols = slice(i * wide, (i + 1) * wide)
        total = sums[2 * i][...] + decode(sums[2 * i + 1])
        coded, power = encode_rows(total[rows:])
        for p, ref in enumerate(send_refs):
            ref[:, cols] = coded[p * rows : (p + 1) * rows]
            ref[:, width + i * DH : width + (i + 1) * DH] = power[p * rows : (p + 1) * rows]
        keep_ref[:, cols] = total[:rows]


def join_kernel(kept_ref, *refs):
    rows, width = kept_ref.shape
    wide = width // (2 * PARTS)
    parts = []
    for i in range(2 * PARTS):
        cols = slice(i * wide, (i + 1) * wide)
        total = kept_ref[:, cols]
        for ref in refs[:-1]:
            total = total + decode_rows(ref[:, cols], ref[:, width + i * DH : width + (i + 1) * DH])
        parts.append(total)
    total = jnp.concatenate(parts, axis=1)
    rows, wide = rows // NZ, width // 4
    for z in range(NZ):
        mine = total[z * rows : (z + 1) * rows]
        mine = jnp.concatenate([mine[:, q * wide : (q + 1) * wide] for q in range(4)], axis=0)
        refs[-1][z, :, :wide], refs[-1][z, :, wide:] = encode_rows(mine)


def z_kernel(got_ref, out_ref):
    wide = got_ref.shape[2] - DH
    total = None
    for z in range(NZ):
        piece = decode_rows(got_ref[z, :, :wide], got_ref[z, :, wide:])
        total = piece if z == 0 else total + piece
    rows = out_ref.shape[0]
    for q in range(4):
        out_ref[:, q * wide : (q + 1) * wide] = total[q * rows : (q + 1) * rows]


def copy_all(copies):
    for cp in copies:
        cp.start()
    for cp in copies:
        cp.wait()


def halves_kernel(coords_ref, q_ref, g_ref, out_ref, sems):
    tokens, width = q_ref.shape
    at = pl.multiple_of((1 - coords_ref[3]) * (width // NC), width // NC)
    copy_all(
        [
            pltpu.make_async_copy(ref.at[:, pl.ds(at, width // NC)], out_ref.at[pl.ds(i * tokens, tokens)], sems.at[i])
            for i, ref in enumerate((q_ref, g_ref))
        ]
    )


def place_kernel(coords_ref, *refs):
    srcs, (att_ref, dq_ref, sems) = refs[: 2 * PARTS], refs[2 * PARTS :]
    tokens, width = att_ref.shape
    wide = width // NC // PARTS
    copies = []
    for i, src in enumerate(srcs):
        core = coords_ref[3] if i < PARTS else 1 - coords_ref[3]
        at = pl.multiple_of(core * (width // NC) + i % PARTS * wide, wide)
        for j, dst in enumerate((att_ref, dq_ref)):
            copies.append(
                pltpu.make_async_copy(
                    src.at[pl.ds(j * tokens, tokens)], dst.at[:, pl.ds(at, wide)], sems.at[2 * i + j]
                )
            )
    copy_all(copies)


def local(kernel, name, out_shape, *args, coords=None, copies=0):
    space = pl.BlockSpec(memory_space=pl.ANY if copies else pltpu.VMEM)
    smem = [] if coords is None else [pl.BlockSpec(memory_space=pltpu.SMEM)]
    return pl.pallas_call(
        kernel,
        in_specs=smem + [space] * len(args),
        out_specs=jax.tree.map(lambda _: space, out_shape),
        out_shape=out_shape,
        scratch_shapes=[pltpu.SemaphoreType.DMA((copies,))] if copies else [],
        compiler_params=pltpu.CompilerParams(vmem_limit_bytes=16 * 2**20),
        name=name,
    )(*([] if coords is None else [coords]), *args)


def fetch(coords, neighbour_ids, entry_home, cache):
    ents = cache.shape[0]
    vmem = pl.BlockSpec(memory_space=pltpu.VMEM)
    smem = pl.BlockSpec(memory_space=pltpu.SMEM)
    pieces = pl.pallas_call(
        spread_kernel,
        in_specs=[smem, smem, smem, pl.BlockSpec(memory_space=pl.ANY)],
        out_specs=vmem,
        out_shape=jax.ShapeDtypeStruct((RB * FB, ents + 1, TILE_R, DH), jnp.bfloat16),
        scratch_shapes=[pltpu.SemaphoreType.DMA((RB * FB,))],
        compiler_params=pltpu.CompilerParams(vmem_limit_bytes=16 * 2**20),
        name="spread",
    )(
        coords,
        *(pltpu.with_memory_space_constraint(a, pltpu.HBM) for a in (neighbour_ids.T, entry_home, cache)),
    )
    store = lax.all_to_all(pieces, PLANE, split_axis=0, concat_axis=0, tiled=True)
    spots = store[:, ents, 0, :WANT].astype(jnp.int32)
    picked = pl.pallas_call(
        pick_kernel,
        in_specs=[smem, vmem],
        out_specs=vmem,
        out_shape=jax.ShapeDtypeStruct((N_DB * WANT, TILE_R, DH), jnp.bfloat16),
        compiler_params=pltpu.CompilerParams(vmem_limit_bytes=16 * 2**20),
        name="pick",
    )(spots, store)
    picked, coords = lax.optimization_barrier((picked, coords))
    answer = lax.all_to_all(
        picked.reshape(N_DB, WANT, TILE_R, DH), PLANE, split_axis=0, concat_axis=0, tiled=True
    )
    return answer, coords


def hops(mask, second):
    out = []
    for y in range(NY):
        for x in range(NX):
            for c in range(NC):
                to = (y, x ^ mask) if c == second else (y ^ mask, x)
                out.append(((y * NX + x) * NC + c, (to[0] * NX + to[1]) * NC + c))
    return out


def body(queries, grad_out, neighbour_ids, entry_home, cache, kv_weight):
    coords = jnp.stack([lax.axis_index(axis).astype(jnp.int32) for axis in ALL])
    tokens, width = queries.shape
    shape = jax.ShapeDtypeStruct
    swap = lambda v: lax.ppermute(v, "core", [(0, 1), (1, 0)])
    answer, coords = fetch(coords, neighbour_ids, entry_home, cache)
    hbm = lambda v: pltpu.with_memory_space_constraint(v, pltpu.HBM)
    theirs = shape((2 * tokens, width // NC), queries.dtype)
    oth = swap(local(halves_kernel, "halves", theirs, hbm(queries), hbm(grad_out), coords=coords, copies=2))
    half, quarter = FEAT // 2, FEAT // 4
    wide = width // NC // PARTS
    folded = [shape((quarter, wide), jnp.float32), shape((quarter + TILE_R, wide), jnp.int16)]
    tie = lax.optimization_barrier

    def one(keep_k, send_k, keep_v, send_v):
        return [keep_k, lax.ppermute(send_k, PLANE, hops(1, 0)), keep_v, lax.ppermute(send_v, PLANE, hops(3, 0))]

    def two(keep_k, came_k, keep_v, came_v):
        out = []
        for kept, came, mask in ((keep_k, came_k, 3), (keep_v, came_v, 1)):
            kept, sent = local(fold_kernel, "fold", folded, kept, came)
            out += [kept, lax.ppermute(sent, PLANE, hops(mask, 0))]
        return out

    args = (queries, grad_out, oth, kv_weight)
    own, other, *grads = attend(coords, (answer, swap(answer)), *args)
    sums = one(*grads)
    other = swap(other)
    sums = two(*sums)
    outs = [shape(queries.shape, queries.dtype)] * 2
    outs = local(place_kernel, "place", outs, own, other, coords=coords, copies=4)
    sums[3], outs = tie((sums[3], outs))
    part = quarter // 4
    shapes = [shape((part, width), jnp.float32)]
    shapes += [shape((part, width + 2 * PARTS * DH), jnp.int16)] * 3
    kept, *sent = local(split_kernel, "split", shapes, *sums)
    came = [lax.ppermute(v, PLANE, hops(mask, 1)) for v, mask in zip(sent, RING[1:])]
    pieces = local(join_kernel, "join", shape((NZ, 4 * part // NZ, width // 4 + DH), jnp.int16), kept, *came)
    got = lax.all_to_all(pieces, "z", split_axis=0, concat_axis=0, tiled=True)
    total = local(z_kernel, "zsum", shape((2 * NC, width), jnp.float32), got)
    core = lax.axis_index("core")
    mine = lax.dynamic_slice(total, (2 * core, 0), (2, width))
    came = swap(lax.dynamic_slice(total, (2 - 2 * core, 0), (2, width)))
    low, high = jnp.where(core == 0, mine, came), jnp.where(core == 0, came, mine)
    weight_grad = jnp.concatenate(
        [low[:, : width // 2], high[:, : width // 2], low[:, width // 2 :], high[:, width // 2 :]], axis=1
    )
    return (*outs, weight_grad)


def solution(mesh):
    grid = Mesh(mesh.devices.reshape(NZ, NY, NX, NC), ALL)
    return jax.shard_map(
        body,
        mesh=grid,
        in_specs=(P(ALL, None), P(ALL, None), P(ALL, None), P(), P(PLANE, None, None), P()),
        out_specs=(P(ALL, None), P(ALL, None), P(ALL, None)),
        check_vma=False,
    )
```

time: 445 us -> 128 us (0.29)
  waiting for transfers between devices: 320 us -> 44.2 us
  matrix products: 50 us -> 0 us
  local copies, waits for them, and re-layouts: 32.1 us -> 0.02 us
  Pallas kernels: 0 us -> 30.4 us
  starting transfers between devices: 5.25 us -> 24 us
  between operations: 14.3 us -> 0.76 us
  blocking collectives: 15.3 us -> 27.3 us
  other arithmetic: 7.31 us -> 0.74 us
    unnamed x2 -> x0, waiting for transfers between devices: 270 us -> none
    dot_general x8 -> x0, matrix products: 50 us -> none  [the longest x1 13.6 us: attention_pass(): jnp.einsum('chqk,ckhd->cqhd', probs_b, values, preferred_element_type=jnp...]
    pallas_call x0 -> x10, Pallas kernels: none -> 30.4 us  [the longest x1 20.1 us: attend(): pl.pallas_call(first_kernel, grid_spec=pltpu.PrefetchScalarGridSpec(num_s...]
    all_to_all x1 -> x2, waiting for transfers between devices: 49.8 us -> 23.5 us  [the longest x1 15.1 us: fetch(): lax.all_to_all(picked.reshape(N_DB, WANT, TILE_R, DH), PLANE, split_axis=...]
    ppermute x0 -> x11, waiting for transfers between devices: none -> 20.7 us  [the longest x1 9.32 us: one(): lax.ppermute(send_v, PLANE, hops(3, 0))]
    all_to_all x1, blocking collectives: 15.3 us -> 27.3 us  [fetch(): lax.all_to_all(pieces, PLANE, split_axis=0, concat_axis=0, tiled=True)]
    ppermute x0 -> x11, starting transfers between devices: none -> 11.8 us  [the longest x4 6.12 us: body(): swap = lambda v: lax.ppermute(v, 'core', [(0, 1), (1, 0)])]
    unnamed x29 -> x0, local copies, waits for them, and re-layouts: 10.7 us -> none
  transfers between devices with their start and end apart: 2 -> 13, of which waited for: 2 -> 9; matrix products, arithmetic and copies ran while one was open for 2% -> 0% of each run, Pallas kernels for 0% -> 3%
where the time goes in v1:
time: 128 us; the launch traced here: 127 us
  waiting for transfers between devices  44.2 us (35%)
  Pallas kernels  30.4 us (24%)
  blocking collectives  27.3 us (21%)
  starting transfers between devices  24 us (19%)
    all_to_all x1, blocking collectives, fetch(): lax.all_to_all(pieces, PLANE, split_axis=0, concat_axis=0, tiled=True)  27.3 us
    pallas_call x1, Pallas kernels, attend(): pl.pallas_call(first_kernel, grid_spec=pltpu.PrefetchScalarGridSpec(num_s...  20.1 us
    all_to_all x1, waiting for transfers between devices, fetch(): lax.all_to_all(picked.reshape(N_DB, WANT, TILE_R, DH), PLANE, split_axis=...  15.1 us
    ppermute x1, waiting for transfers between devices, one(): lax.ppermute(send_v, PLANE, hops(3, 0))  9.32 us
    all_to_all x1, waiting for transfers between devices, body(): got = lax.all_to_all(pieces, 'z', split_axis=0, concat_axis=0, tiled=True)  8.38 us
    all_to_all x1, starting transfers between devices, body(): got = lax.all_to_all(pieces, 'z', split_axis=0, concat_axis=0, tiled=True)  8.18 us
    ppermute x4, starting transfers between devices, body(): swap = lambda v: lax.ppermute(v, 'core', [(0, 1), (1, 0)])  6.12 us
    pallas_call x7, Pallas kernels, local(): pl.pallas_call(kernel, in_specs=smem + [space] * len(args), out_specs=jax...  5.69 us
  transfers between devices with their start and end apart: 13, of which 9 were waited for; matrix products, arithmetic and copies ran while one was open for 0% of the time, Pallas kernels for 3%

profile of v1, /device:TPU:1, one launch (start us, length us, event | category | flops | bytes accessed | tf_op | source)
XLA Modules:
  0.0 127.3 jit_solution(8234478524602575231)
XLA Ops:
  0.6 0.1 pad_add_fusion.coords_ref
  0.7 2.2 %spread.1 = bf16[32,9,16,128]{3,2,1,0:T(8,128)(2,1)S(1)} custom-call(s32[4]{0:T(128)S(1)} %pad_add_fusion.coords_ref, s32[2,4]{1,0:T(2,128)} %bitcast.8, s32[256]{0:T(256)} %home_ref.1, bf16[8,128,512]{2,1,0:T(8,128)(2,1)} %cache_ref.1), custom_call_target="tpu_custom_call" | custom-call | tf_op jit(solution)/shard_map/spread/pallas_call | solution.py:364
  2.9 27.3 %all_to_all.15.store_ref = bf16[32,9,16,128]{3,2,1,0:T(8,128)(2,1)S(1)} all-to-all(bf16[32,9,16,128]{3,2,1,0:T(8,128)(2,1)S(1)} %spread.1), channel_id=1, replica_groups=mesh['z'=8,'y'=4,'x'=4,'core'=2] {'y','x','core'}, dimensions={0} | all-to-all | bytes 2359296 | tf_op jit(solution)/shard_map/all_to_all | solution.py:376
  30.2 2.4 %pick.1 = bf16[256,16,128]{2,1,0:T(8,128)(2,1)} custom-call(s32[32,8]{1,0:T(8,128)S(1)} %bitcast.7, bf16[32,9,16,128]{3,2,1,0:T(8,128)(2,1)S(1)} %all_to_all.15.store_ref), custom_call_target="tpu_custom_call" | custom-call | tf_op jit(solution)/shard_map/pick/pallas_call | solution.py:378
  32.6 4.0 %all-to-all-start.1 = ((bf16[32,8,16,128]{3,2,1,0:T(8,128)(2,1)}), bf16[32,8,16,128]{3,2,1,0:T(8,128)(2,1)S(1)}, u32[]{:S(2)}, u32[]{:S(2)}) async-start(bf16[32,8,16,128]{3,2,1,0:T(8,128)(2,1)} %bitcast.6), calls=%async_computation.1 | async-start | bytes 2097152 | tf_op jit(solution)/shard_map/all_to_all | solution.py:387
  36.6 1.8 %halves.1 = bf16[512,1024]{1,0:T(8,128)(2,1)S(1)} custom-call(s32[4]{0:T(128)S(1)} %pad_add_fusion.coords_ref, bf16[256,2048]{1,0:T(8,128)(2,1)} %q_ref.3, bf16[256,2048]{1,0:T(8,128)(2,1)} %g_ref.3), custom_call_target="tpu_custom_call" | custom-call | tf_op jit(solution)/shard_map/halves/pallas_call | solution.py:349
  38.4 0.4 collective-permute-start.1
  38.8 15.1 %all-to-all-done.1.r_ref = bf16[32,8,16,128]{3,2,1,0:T(8,128)(2,1)S(1)} async-done(((bf16[32,8,16,128]{3,2,1,0:T(8,128)(2,1)}), bf16[32,8,16,128]{3,2,1,0:T(8,128)(2,1)S(1)}, u32[]{:S(2)}, u32[]{:S(2)}) %all-to-all-start.1) | async-done | bytes 1048608 | tf_op jit(solution)/shard_map/all_to_all | solution.py:387
  53.9 0.4 collective-permute-start
  54.3 0.0 collective-permute-done.1.qg_ref
  54.3 2.3 %collective-permute-done.rr_ref = bf16[32,8,16,128]{3,2,1,0:T(8,128)(2,1)S(1)} collective-permute-done((bf16[32,8,16,128]{3,2,1,0:T(8,128)(2,1)S(1)}, bf16[32,8,16,128]{3,2,1,0:T(8,128)(2,1)S(1)}, u32[]{:S(2)}, u32[]{:S(2)}) %collective-permute-start) | collective-permute-done | bytes 1048608 | tf_op jit(solution)/shard_map/ppermute | solution.py:407
  56.6 20.1 %attend.1 = (bf16[512,1024]{1,0:T(8,128)(2,1)S(1)}, bf16[512,1024]{1,0:T(8,128)(2,1)S(1)}, f32[256,1024]{1,0:T(8,128)S(1)}, s16[272,1024]{1,0:T(8,128)(2,1)S(1)}...) custom-call(s32[4]{0:T(128)S(1)} %pad_add_fusion.coords_ref, bf16[32,8,16,128]{3,2,1,0:T(8,128)(2,1)S(1)} %all-to-all-done.1.r_ref, ...), custom_call_target="tpu_custom_call" | custom-call | flops 11000000512 | bytes 8388608 | tf_op jit(solution)/shard_map/attend/pallas_call | solution.py:232
  76.7 0.5 collective-permute-start.4
  77.1 0.6 collective-permute-start.2
  77.7 0.0 collective-permute-start.5
  77.7 9.3 %collective-permute-done.2.came_ref = s16[272,1024]{1,0:T(8,128)(2,1)S(1)} collective-permute-done((s16[272,1024]{1,0:T(8,128)(2,1)S(1)}, s16[272,1024]{1,0:T(8,128)(2,1)S(1)}, u32[]{:S(2)}, u32[]{:S(2)}) %collective-permute-start.2) | collective-permute-done | bytes 557088 | tf_op jit(solution)/shard_map/ppermute | solution.py:418
  87.0 0.3 fold.2
  87.3 0.1 collective-permute-start.3
  87.4 0.0 collective-permute-done.5.came_ref
  87.5 0.3 fold.3
  87.8 1.1 collective-permute-start.6
  88.9 0.0 collective-permute-done.4.refs_1_
  88.9 1.9 %place.1 = (bf16[256,2048]{1,0:T(8,128)(2,1)}, bf16[256,2048]{1,0:T(8,128)(2,1)}) custom-call(s32[4]{0:T(128)S(1)} %pad_add_fusion.coords_ref, bf16[512,1024]{1,0:T(8,128)(2,1)S(1)} %get-tuple-element.29.refs_0_, bf16[512,1024]{1,0:T(8,128)(2,1)S(1)} %collective-permute-done.4.refs_1_), custom_call_target="tpu_custom_call" | custom-call | tf_op jit(solution)/shard_map/place/pallas_call | solution.py:349
  90.8 2.5 %collective-permute-done.3.refs_3_ = s16[144,1024]{1,0:T(8,128)(2,1)S(1)} collective-permute-done((s16[144,1024]{1,0:T(8,128)(2,1)S(1)}, s16[144,1024]{1,0:T(8,128)(2,1)S(1)}, u32[]{:S(2)}, u32[]{:S(2)}) %collective-permute-start.3) | collective-permute-done | bytes 294944 | tf_op jit(solution)/shard_map/ppermute | solution.py:424
  93.3 1.7 %collective-permute-done.6.refs_1_ = s16[144,1024]{1,0:T(8,128)(2,1)S(1)} collective-permute-done((s16[144,1024]{1,0:T(8,128)(2,1)S(1)}, s16[144,1024]{1,0:T(8,128)(2,1)S(1)}, u32[]{:S(2)}, u32[]{:S(2)}) %collective-permute-start.6) | collective-permute-done | bytes 294944 | tf_op jit(solution)/shard_map/ppermute | solution.py:424
  95.0 0.3 split.1
  95.3 1.3 collective-permute-start.7
  96.6 0.0 collective-permute-start.8
  96.6 2.7 %collective-permute-start.9 = (s16[32,2304]{1,0:T(8,128)(2,1)S(1)}, s16[32,2304]{1,0:T(8,128)(2,1)S(1)}, u32[]{:S(2)}, u32[]{:S(2)}) collective-permute-start(s16[32,2304]{1,0:T(8,128)(2,1)S(1)} %get-tuple-element.44), channel_id=1, source_target_pairs={{0,16},{1,5},{2,18},{3,7},{4,20},{5,1},{6,22},{7,3},{8,24},{9,13},... | collective-permute-start | bytes 442376 | tf_op jit(solution)/shard_map/ppermute | solution.py:439
  99.3 1.3 %collective-permute-done.7.refs_0_ = s16[32,2304]{1,0:T(8,128)(2,1)S(1)} collective-permute-done((s16[32,2304]{1,0:T(8,128)(2,1)S(1)}, s16[32,2304]{1,0:T(8,128)(2,1)S(1)}, u32[]{:S(2)}, u32[]{:S(2)}) %collective-permute-start.7) | collective-permute-done | bytes 147488 | tf_op jit(solution)/shard_map/ppermute | solution.py:439
  100.6 0.0 collective-permute-done.8.refs_1_
  100.6 2.8 %collective-permute-done.9.refs_2_ = s16[32,2304]{1,0:T(8,128)(2,1)S(1)} collective-permute-done((s16[32,2304]{1,0:T(8,128)(2,1)S(1)}, s16[32,2304]{1,0:T(8,128)(2,1)S(1)}, u32[]{:S(2)}, u32[]{:S(2)}) %collective-permute-start.9) | collective-permute-done | bytes 147488 | tf_op jit(solution)/shard_map/ppermute | solution.py:439
  103.4 0.9 join.1
  104.3 8.2 %all-to-all-start.2 = ((s16[8,16,640]{2,1,0:T(8,128)(2,1)}), s16[8,16,640]{2,1,0:T(8,128)(2,1)S(1)}, u32[]{:S(2)}, u32[]{:S(2)}) async-start(s16[8,16,640]{2,1,0:T(8,128)(2,1)} %join.1), calls=%async_computation.2 | async-start | bytes 327680 | tf_op jit(solution)/shard_map/all_to_all | solution.py:441
  112.5 8.4 %all-to-all-done.2.got_ref = s16[8,16,640]{2,1,0:T(8,128)(2,1)S(1)} async-done(((s16[8,16,640]{2,1,0:T(8,128)(2,1)}), s16[8,16,640]{2,1,0:T(8,128)(2,1)S(1)}, u32[]{:S(2)}, u32[]{:S(2)}) %all-to-all-start.2) | async-done | bytes 163872 | tf_op jit(solution)/shard_map/all_to_all | solution.py:441
  120.9 0.1 zsum.1
  121.0 4.8 %collective-permute-start.10 = (f32[2,2048]{1,0:T(2,128)S(1)}, f32[2,2048]{1,0:T(2,128)S(1)}, u32[]{:S(2)}, u32[]{:S(2)}) collective-permute-start(f32[2,2048]{1,0:T(2,128)S(1)} %constant_dynamic-slice_fusion), channel_id=1, source_target_pairs={{0,1},{1,0},{2,3},{3,2},{4,5},{5,4},{6,7},{7,6},{8,9},{9,8},{10,11... | collective-permute-start | bytes 49160 | tf_op jit(solution)/shard_map/ppermute | solution.py:407
  125.8 0.8 collective-permute-done.10
  126.7 0.6 pad_maximum_fusion
  (4 shorter events, 0.0 us)
Async XLA Ops:
  32.6 21.3 %all-to-all-start.1 = ((bf16[32,8,16,128]{3,2,1,0:T(8,128)(2,1)}), bf16[32,8,16,128]{3,2,1,0:T(8,128)(2,1)S(1)}, u32[]{:S(2)}, u32[]{:S(2)}) async-start(bf16[32,8,16,128]{3,2,1,0:T(8,128)(2,1)} %bitcast.6), calls=%async_computation.1 | async-start | bytes 2097152 | tf_op jit(solution)/shard_map/all_to_all | solution.py:387
  38.4 15.9 %collective-permute-start.1 = (bf16[512,1024]{1,0:T(8,128)(2,1)S(1)}, bf16[512,1024]{1,0:T(8,128)(2,1)S(1)}, u32[]{:S(2)}, u32[]{:S(2)}) collective-permute-start(bf16[512,1024]{1,0:T(8,128)(2,1)S(1)} %halves.1), channel_id=1, source_target_pairs={{0,1},{1,0},{2,3},{3,2},{4,5},{5,4},{6,7},{7,6},{8,9},{9,8},{10,11... | collective-permute-start | bytes 3145736 | tf_op jit(solution)/shard_map/ppermute | solution.py:407
  53.9 2.7 %collective-permute-start = (bf16[32,8,16,128]{3,2,1,0:T(8,128)(2,1)S(1)}, bf16[32,8,16,128]{3,2,1,0:T(8,128)(2,1)S(1)}, u32[]{:S(2)}, u32[]{:S(2)}) collective-permute-start(bf16[32,8,16,128]{3,2,1,0:T(8,128)(2,1)S(1)} %all-to-all-done.1.r_ref), channel_id=1, source_target_pairs={{0,1},{1,0},{2,3},{3,2},{4,5},{5,4},{6,7},{7,6},{8,9},{9,8},{10,11... | collective-permute-start | bytes 3145736 | tf_op jit(solution)/shard_map/ppermute | solution.py:407
  76.7 12.2 %collective-permute-start.4 = (bf16[512,1024]{1,0:T(8,128)(2,1)S(1)}, bf16[512,1024]{1,0:T(8,128)(2,1)S(1)}, u32[]{:S(2)}, u32[]{:S(2)}) collective-permute-start(bf16[512,1024]{1,0:T(8,128)(2,1)S(1)} %get-tuple-element.30), channel_id=1, source_target_pairs={{0,1},{1,0},{2,3},{3,2},{4,5},{5,4},{6,7},{7,6},{8,9},{9,8},{10,11... | collective-permute-start | bytes 3145736 | tf_op jit(solution)/shard_map/ppermute | solution.py:407
  77.1 9.9 %collective-permute-start.2 = (s16[272,1024]{1,0:T(8,128)(2,1)S(1)}, s16[272,1024]{1,0:T(8,128)(2,1)S(1)}, u32[]{:S(2)}, u32[]{:S(2)}) collective-permute-start(s16[272,1024]{1,0:T(8,128)(2,1)S(1)} %get-tuple-element.27), channel_id=1, source_target_pairs={{0,6},{1,25},{2,4},{3,27},{4,2},{5,29},{6,0},{7,31},{8,14},{9,17},... | collective-permute-start | bytes 1671176 | tf_op jit(solution)/shard_map/ppermute | solution.py:418
  77.7 9.8 %collective-permute-start.5 = (s16[272,1024]{1,0:T(8,128)(2,1)S(1)}, s16[272,1024]{1,0:T(8,128)(2,1)S(1)}, u32[]{:S(2)}, u32[]{:S(2)}) collective-permute-start(s16[272,1024]{1,0:T(8,128)(2,1)S(1)} %get-tuple-element.36), channel_id=1, source_target_pairs={{0,2},{1,9},{2,0},{3,11},{4,6},{5,13},{6,4},{7,15},{8,10},{9,1},{1... | collective-permute-start | bytes 1671176 | tf_op jit(solution)/shard_map/ppermute | solution.py:418
  87.3 6.0 %collective-permute-start.3 = (s16[144,1024]{1,0:T(8,128)(2,1)S(1)}, s16[144,1024]{1,0:T(8,128)(2,1)S(1)}, u32[]{:S(2)}, u32[]{:S(2)}) collective-permute-start(s16[144,1024]{1,0:T(8,128)(2,1)S(1)} %get-tuple-element.28), channel_id=1, source_target_pairs={{0,2},{1,9},{2,0},{3,11},{4,6},{5,13},{6,4},{7,15},{8,10},{9,1},{1... | collective-permute-start | bytes 884744 | tf_op jit(solution)/shard_map/ppermute | solution.py:424
  87.8 7.2 %collective-permute-start.6 = (s16[144,1024]{1,0:T(8,128)(2,1)S(1)}, s16[144,1024]{1,0:T(8,128)(2,1)S(1)}, u32[]{:S(2)}, u32[]{:S(2)}) collective-permute-start(s16[144,1024]{1,0:T(8,128)(2,1)S(1)} %get-tuple-element.38), channel_id=1, source_target_pairs={{0,6},{1,25},{2,4},{3,27},{4,2},{5,29},{6,0},{7,31},{8,14},{9,17},... | collective-permute-start | bytes 884744 | tf_op jit(solution)/shard_map/ppermute | solution.py:424
  95.3 5.3 %collective-permute-start.7 = (s16[32,2304]{1,0:T(8,128)(2,1)S(1)}, s16[32,2304]{1,0:T(8,128)(2,1)S(1)}, u32[]{:S(2)}, u32[]{:S(2)}) collective-permute-start(s16[32,2304]{1,0:T(8,128)(2,1)S(1)} %get-tuple-element.42), channel_id=1, source_target_pairs={{0,24},{1,7},{2,26},{3,5},{4,28},{5,3},{6,30},{7,1},{8,16},{9,15},... | collective-permute-start | bytes 442376 | tf_op jit(solution)/shard_map/ppermute | solution.py:439
  96.6 4.0 %collective-permute-start.8 = (s16[32,2304]{1,0:T(8,128)(2,1)S(1)}, s16[32,2304]{1,0:T(8,128)(2,1)S(1)}, u32[]{:S(2)}, u32[]{:S(2)}) collective-permute-start(s16[32,2304]{1,0:T(8,128)(2,1)S(1)} %get-tuple-element.43), channel_id=1, source_target_pairs={{0,8},{1,3},{2,10},{3,1},{4,12},{5,7},{6,14},{7,5},{8,0},{9,11},{1... | collective-permute-start | bytes 442376 | tf_op jit(solution)/shard_map/ppermute | solution.py:439
  96.6 6.8 %collective-permute-start.9 = (s16[32,2304]{1,0:T(8,128)(2,1)S(1)}, s16[32,2304]{1,0:T(8,128)(2,1)S(1)}, u32[]{:S(2)}, u32[]{:S(2)}) collective-permute-start(s16[32,2304]{1,0:T(8,128)(2,1)S(1)} %get-tuple-element.44), channel_id=1, source_target_pairs={{0,16},{1,5},{2,18},{3,7},{4,20},{5,1},{6,22},{7,3},{8,24},{9,13},... | collective-permute-start | bytes 442376 | tf_op jit(solution)/shard_map/ppermute | solution.py:439
  104.3 16.6 %all-to-all-start.2 = ((s16[8,16,640]{2,1,0:T(8,128)(2,1)}), s16[8,16,640]{2,1,0:T(8,128)(2,1)S(1)}, u32[]{:S(2)}, u32[]{:S(2)}) async-start(s16[8,16,640]{2,1,0:T(8,128)(2,1)} %join.1), calls=%async_computation.2 | async-start | bytes 327680 | tf_op jit(solution)/shard_map/all_to_all | solution.py:441
  121.0 5.7 %collective-permute-start.10 = (f32[2,2048]{1,0:T(2,128)S(1)}, f32[2,2048]{1,0:T(2,128)S(1)}, u32[]{:S(2)}, u32[]{:S(2)}) collective-permute-start(f32[2,2048]{1,0:T(2,128)S(1)} %constant_dynamic-slice_fusion), channel_id=1, source_target_pairs={{0,1},{1,0},{2,3},{3,2},{4,5},{5,4},{6,7},{7,6},{8,9},{9,8},{10,11... | collective-permute-start | bytes 49160 | tf_op jit(solution)/shard_map/ppermute | solution.py:407

commit v2 on v1

--- a/solution.py
+++ b/solution.py
@@ -30,8 +30,12 @@
 PLANE = ("y", "x", "core")
 
 
-def spread_kernel(coords_ref, ids_ref, home_ref, cache_ref, out_ref, sems):
+def spread_kernel(coords_ref, ids_hbm, home_hbm, cache_ref, out_ref, ids_ref, home_ref, sems):
     ents = cache_ref.shape[0]
+    small = [
+        pltpu.make_async_copy(ids_hbm, ids_ref, sems.at[RB * FB]),
+        pltpu.make_async_copy(home_hbm, home_ref, sems.at[RB * FB + 1]),
+    ]
     copies = []
     for rb in range(RB):
         for fb in range(FB):
@@ -43,8 +47,10 @@
                     sems.at[m],
                 )
             )
-    for cp in copies:
+    for cp in small + copies:
         cp.start()
+    for cp in small:
+        cp.wait()
     row = lax.broadcasted_iota(jnp.int32, (TILE_R, DH), 0)
     lane = lax.broadcasted_iota(jnp.int32, (TILE_R, DH), 1)
     tile = jnp.zeros((TILE_R, DH), jnp.float32)
@@ -118,32 +124,27 @@
     return jnp.where(new == place, 1.0, 0.0).astype(jnp.bfloat16)
 
 
-def lay_rows(coords_ref, r_ref, rr_ref, f_ref, ft_ref, sems):
-    copies = []
-    for side, ref in enumerate((r_ref, rr_ref)):
+def lay_rows(coords_ref, r_ref, rr_refs, f_ref, ft_ref):
+    half = RB * FB // 2
+    for side in range(NC):
         for rb in range(RB):
             for fb in range(FB):
                 m = rb * FB + fb
-                copies.append(
-                    pltpu.make_async_copy(
-                        ref.at[m],
-                        f_ref.at[pl.ds(side * WANT, WANT), rb, :, fb * DH : (fb + 1) * DH],
-                        sems.at[side * RB * FB + m],
-                    )
-                )
-    copy_all(copies)
+                ref, at = (r_ref, m) if side == 0 else (rr_refs[m // half], m % half)
+                for w in range(WANT):
+                    f_ref[side * WANT + w, rb, :, fb * DH : (fb + 1) * DH] = ref[at, w]
     f = f_ref[...].reshape(NC * WANT * ROWS, FEAT)
     ft_ref[...] = lax.dot_general(row_order(coords_ref), f, NT, preferred_element_type=jnp.float32).astype(
         jnp.bfloat16
     )
 
 
-def first_kernel(coords_ref, r_ref, rr_ref, q_ref, g_ref, qg_ref, wk_ref, wv_ref, *refs):
-    outs, f_ref, ft_ref, scratch, sems = refs[:6], refs[6], refs[7], refs[8:-1], refs[-1]
+def first_kernel(coords_ref, r_ref, rr0_ref, rr1_ref, q_ref, g_ref, qg_ref, wk_ref, wv_ref, *refs):
+    outs, f_ref, ft_ref, scratch = refs[:6], refs[6], refs[7], refs[8:]
 
     @pl.when(pl.program_id(0) == 0)
     def _():
-        lay_rows(coords_ref, r_ref, rr_ref, f_ref, ft_ref, sems)
+        lay_rows(coords_ref, r_ref, (rr0_ref, rr1_ref), f_ref, ft_ref)
 
     attend_kernel(coords_ref, f_ref, ft_ref, q_ref, g_ref, qg_ref, wk_ref, wv_ref, *outs, *scratch)
 
@@ -234,7 +235,7 @@
         grid_spec=pltpu.PrefetchScalarGridSpec(
             num_scalar_prefetch=1,
             grid=(steps,),
-            in_specs=[pl.BlockSpec(memory_space=pl.ANY)] * 2
+            in_specs=[pl.BlockSpec(memory_space=pltpu.VMEM)] * 3
             + [mine(tokens, 0), mine(tokens, 0), col(2 * tokens), mine(FEAT, 0), mine(FEAT, NC * steps)],
             out_specs=[
                 col(2 * tokens), col(2 * tokens),
@@ -244,8 +245,7 @@
                 pltpu.VMEM((NC * WANT, RB, TILE_R, FEAT), jnp.bfloat16),
                 pltpu.VMEM((FEAT, every), jnp.bfloat16),
             ]
-            + [pltpu.VMEM((every, WIDE), jnp.bfloat16)] * 4
-            + [pltpu.SemaphoreType.DMA((NC * RB * FB,))],
+            + [pltpu.VMEM((every, WIDE), jnp.bfloat16)] * 4,
         ),
         out_shape=[
             shape(2 * tokens, jnp.bfloat16), shape(2 * tokens, jnp.bfloat16),
@@ -363,10 +363,14 @@
     smem = pl.BlockSpec(memory_space=pltpu.SMEM)
     pieces = pl.pallas_call(
         spread_kernel,
-        in_specs=[smem, smem, smem, pl.BlockSpec(memory_space=pl.ANY)],
+        in_specs=[pl.BlockSpec(memory_space=pl.ANY)] * 4,
         out_specs=vmem,
         out_shape=jax.ShapeDtypeStruct((RB * FB, ents + 1, TILE_R, DH), jnp.bfloat16),
-        scratch_shapes=[pltpu.SemaphoreType.DMA((RB * FB,))],
+        scratch_shapes=[
+            pltpu.SMEM(neighbour_ids.shape[::-1], jnp.int32),
+            pltpu.SMEM(entry_home.shape, jnp.int32),
+            pltpu.SemaphoreType.DMA((RB * FB + 2,)),
+        ],
         compiler_params=pltpu.CompilerParams(vmem_limit_bytes=16 * 2**20),
         name="spread",
     )(
@@ -379,7 +383,7 @@
         pick_kernel,
         in_specs=[smem, vmem],
         out_specs=vmem,
-        out_shape=jax.ShapeDtypeStruct((N_DB * WANT, TILE_R, DH), jnp.bfloat16),
+        out_shape=pltpu.VMEM((N_DB * WANT, TILE_R, DH), jnp.bfloat16),
         compiler_params=pltpu.CompilerParams(vmem_limit_bytes=16 * 2**20),
         name="pick",
     )(spots, store)
@@ -425,7 +429,7 @@
         return out
 
     args = (queries, grad_out, oth, kv_weight)
-    own, other, *grads = attend(coords, (answer, swap(answer)), *args)
+    own, other, *grads = attend(coords, (answer, swap(answer[:16]), swap(answer[16:])), *args)
     sums = one(*grads)
     other = swap(other)
     sums = two(*sums)

time: 128 us -> 125 us (0.977)
  Pallas kernels: 30.4 us -> 28.6 us
  starting transfers between devices: 24 us -> 22.5 us
    ppermute x4 -> x5, starting transfers between devices: 6.12 us -> 5.85 us  [body(): swap = lambda v: lax.ppermute(v, 'core', [(0, 1), (1, 0)])]
    ppermute x4 -> x5, waiting for transfers between devices: 3.13 us -> 3.01 us  [body(): swap = lambda v: lax.ppermute(v, 'core', [(0, 1), (1, 0)])]
  transfers between devices with their start and end apart: 13 -> 14, of which waited for: 9 -> 10; matrix products, arithmetic and copies ran while one was open for 0% -> 0% of each run, Pallas kernels for 3% -> 3%
where the time goes in v2:
time: 125 us
  waiting for transfers between devices  44.6 us (36%)
  Pallas kernels  28.6 us (23%)
  blocking collectives  27.3 us (22%)
  starting transfers between devices  22.5 us (18%)
    all_to_all x1, blocking collectives, fetch(): lax.all_to_all(pieces, PLANE, split_axis=0, concat_axis=0, tiled=True)  27.3 us
    pallas_call x1, Pallas kernels, attend(): pl.pallas_call(first_kernel, grid_spec=pltpu.PrefetchScalarGridSpec(num_s...  19.1 us
    all_to_all x1, waiting for transfers between devices, fetch(): lax.all_to_all(picked.reshape(N_DB, WANT, TILE_R, DH), PLANE, split_axis=...  15.1 us
    ppermute x1, waiting for transfers between devices, one(): lax.ppermute(send_v, PLANE, hops(3, 0))  9.31 us
    all_to_all x1, waiting for transfers between devices, body(): got = lax.all_to_all(pieces, 'z', split_axis=0, concat_axis=0, tiled=True)  8.29 us
    all_to_all x1, starting transfers between devices, body(): got = lax.all_to_all(pieces, 'z', split_axis=0, concat_axis=0, tiled=True)  8.18 us
    ppermute x5, starting transfers between devices, body(): swap = lambda v: lax.ppermute(v, 'core', [(0, 1), (1, 0)])  5.85 us
    pallas_call x7, Pallas kernels, local(): pl.pallas_call(kernel, in_specs=smem + [space] * len(args), out_specs=jax...  5.68 us
  transfers between devices with their start and end apart: 14, of which 10 were waited for; matrix products, arithmetic and copies ran while one was open for 0% of the time, Pallas kernels for 3%

profile of v2, /device:TPU:1, one launch (start us, length us, event | category | flops | bytes accessed | tf_op | source)
XLA Modules:
  0.0 124.7 jit_solution(4825778292079743238)
XLA Ops:
  0.6 0.1 pad_add_fusion.coords_ref
  0.7 1.5 %spread.1 = bf16[32,9,16,128]{3,2,1,0:T(8,128)(2,1)S(1)} custom-call(s32[4]{0:T(128)S(1)} %pad_add_fusion.coords_ref, s32[2,4]{1,0:T(2,128)} %bitcast.8, s32[256]{0:T(256)} %home_hbm.1, bf16[8,128,512]{2,1,0:T(8,128)(2,1)} %cache_ref.1), custom_call_target="tpu_custom_call" | custom-call | tf_op jit(solution)/shard_map/spread/pallas_call | solution.py:364
  2.2 27.3 %all_to_all.15.store_ref = bf16[32,9,16,128]{3,2,1,0:T(8,128)(2,1)S(1)} all-to-all(bf16[32,9,16,128]{3,2,1,0:T(8,128)(2,1)S(1)} %spread.1), channel_id=1, replica_groups=mesh['z'=8,'y'=4,'x'=4,'core'=2] {'y','x','core'}, dimensions={0} | all-to-all | bytes 2359296 | tf_op jit(solution)/shard_map/all_to_all | solution.py:380
  29.5 2.4 %pick.1 = bf16[256,16,128]{2,1,0:T(8,128)(2,1)} custom-call(s32[32,8]{1,0:T(8,128)S(1)} %bitcast.7, bf16[32,9,16,128]{3,2,1,0:T(8,128)(2,1)S(1)} %all_to_all.15.store_ref), custom_call_target="tpu_custom_call" | custom-call | tf_op jit(solution)/shard_map/pick/pallas_call | solution.py:382
  31.9 4.0 %all-to-all-start.1 = ((bf16[32,8,16,128]{3,2,1,0:T(8,128)(2,1)}), bf16[32,8,16,128]{3,2,1,0:T(8,128)(2,1)S(1)}, u32[]{:S(2)}, u32[]{:S(2)}) async-start(bf16[32,8,16,128]{3,2,1,0:T(8,128)(2,1)} %bitcast.6), calls=%async_computation.1 | async-start | bytes 2097152 | tf_op jit(solution)/shard_map/all_to_all | solution.py:391
  35.9 1.8 %halves.1 = bf16[512,1024]{1,0:T(8,128)(2,1)S(1)} custom-call(s32[4]{0:T(128)S(1)} %pad_add_fusion.coords_ref, bf16[256,2048]{1,0:T(8,128)(2,1)} %q_ref.3, bf16[256,2048]{1,0:T(8,128)(2,1)} %g_ref.3), custom_call_target="tpu_custom_call" | custom-call | tf_op jit(solution)/shard_map/halves/pallas_call | solution.py:349
  37.7 0.4 collective-permute-start.2
  38.1 15.1 %all-to-all-done.1.r_ref = bf16[32,8,16,128]{3,2,1,0:T(8,128)(2,1)S(1)} async-done(((bf16[32,8,16,128]{3,2,1,0:T(8,128)(2,1)}), bf16[32,8,16,128]{3,2,1,0:T(8,128)(2,1)S(1)}, u32[]{:S(2)}, u32[]{:S(2)}) %all-to-all-start.1) | async-done | bytes 1048608 | tf_op jit(solution)/shard_map/all_to_all | solution.py:391
  53.2 0.2 fusion
  53.4 0.5 collective-permute-start
  53.9 0.1 collective-permute-start.1
  54.0 0.0 collective-permute-done.2.qg_ref
  54.0 1.4 %collective-permute-done.rr0_ref = bf16[16,8,16,128]{3,2,1,0:T(8,128)(2,1)S(1)} collective-permute-done((bf16[16,8,16,128]{3,2,1,0:T(8,128)(2,1)S(1)}, bf16[16,8,16,128]{3,2,1,0:T(8,128)(2,1)S(1)}, u32[]{:S(2)}, u32[]{:S(2)}) %collective-permute-start) | collective-permute-done | bytes 524320 | tf_op jit(solution)/shard_map/ppermute | solution.py:411
  55.4 0.7 collective-permute-done.1.rr1_ref
  56.2 19.1 %attend.1 = (bf16[512,1024]{1,0:T(8,128)(2,1)S(1)}, bf16[512,1024]{1,0:T(8,128)(2,1)S(1)}, f32[256,1024]{1,0:T(8,128)S(1)}, s16[272,1024]{1,0:T(8,128)(2,1)S(1)}...) custom-call(s32[4]{0:T(128)S(1)} %pad_add_fusion.coords_ref, bf16[32,8,16,128]{3,2,1,0:T(8,128)(2,1)S(1)} %all-to-all-done.1.r_ref, ...), custom_call_target="tpu_custom_call" | custom-call | flops 11000000512 | bytes 8388608 | tf_op jit(solution)/shard_map/attend/pallas_call | solution.py:233
  75.2 0.5 collective-permute-start.5
  75.7 0.6 collective-permute-start.3
  76.2 0.0 collective-permute-start.6
  76.3 9.3 %collective-permute-done.3.came_ref = s16[272,1024]{1,0:T(8,128)(2,1)S(1)} collective-permute-done((s16[272,1024]{1,0:T(8,128)(2,1)S(1)}, s16[272,1024]{1,0:T(8,128)(2,1)S(1)}, u32[]{:S(2)}, u32[]{:S(2)}) %collective-permute-start.3) | collective-permute-done | bytes 557088 | tf_op jit(solution)/shard_map/ppermute | solution.py:422
  85.6 0.3 fold.2
  85.9 0.1 collective-permute-start.4
  86.0 0.0 collective-permute-done.6.came_ref
  86.0 0.3 fold.3
  86.4 1.1 collective-permute-start.7
  87.5 0.0 collective-permute-done.5.refs_1_
  87.5 1.9 %place.1 = (bf16[256,2048]{1,0:T(8,128)(2,1)}, bf16[256,2048]{1,0:T(8,128)(2,1)}) custom-call(s32[4]{0:T(128)S(1)} %pad_add_fusion.coords_ref, bf16[512,1024]{1,0:T(8,128)(2,1)S(1)} %get-tuple-element.29.refs_0_, bf16[512,1024]{1,0:T(8,128)(2,1)S(1)} %collective-permute-done.5.refs_1_), custom_call_target="tpu_custom_call" | custom-call | tf_op jit(solution)/shard_map/place/pallas_call | solution.py:349
  89.4 2.5 %collective-permute-done.4.refs_3_ = s16[144,1024]{1,0:T(8,128)(2,1)S(1)} collective-permute-done((s16[144,1024]{1,0:T(8,128)(2,1)S(1)}, s16[144,1024]{1,0:T(8,128)(2,1)S(1)}, u32[]{:S(2)}, u32[]{:S(2)}) %collective-permute-start.4) | collective-permute-done | bytes 294944 | tf_op jit(solution)/shard_map/ppermute | solution.py:428
  91.9 1.7 %collective-permute-done.7.refs_1_ = s16[144,1024]{1,0:T(8,128)(2,1)S(1)} collective-permute-done((s16[144,1024]{1,0:T(8,128)(2,1)S(1)}, s16[144,1024]{1,0:T(8,128)(2,1)S(1)}, u32[]{:S(2)}, u32[]{:S(2)}) %collective-permute-start.7) | collective-permute-done | bytes 294944 | tf_op jit(solution)/shard_map/ppermute | solution.py:428
  93.5 0.3 split.1
  93.9 0.5 collective-permute-start.10
  94.3 1.7 %collective-permute-start.8 = (s16[32,2304]{1,0:T(8,128)(2,1)S(1)}, s16[32,2304]{1,0:T(8,128)(2,1)S(1)}, u32[]{:S(2)}, u32[]{:S(2)}) collective-permute-start(s16[32,2304]{1,0:T(8,128)(2,1)S(1)} %get-tuple-element.42), channel_id=1, source_target_pairs={{0,24},{1,7},{2,26},{3,5},{4,28},{5,3},{6,30},{7,1},{8,16},{9,15},... | collective-permute-start | bytes 442376 | tf_op jit(solution)/shard_map/ppermute | solution.py:443
  96.0 0.6 collective-permute-start.9
  96.6 3.0 %collective-permute-done.10.refs_2_ = s16[32,2304]{1,0:T(8,128)(2,1)S(1)} collective-permute-done((s16[32,2304]{1,0:T(8,128)(2,1)S(1)}, s16[32,2304]{1,0:T(8,128)(2,1)S(1)}, u32[]{:S(2)}, u32[]{:S(2)}) %collective-permute-start.10) | collective-permute-done | bytes 147488 | tf_op jit(solution)/shard_map/ppermute | solution.py:443
  99.6 1.8 %collective-permute-done.8.refs_0_ = s16[32,2304]{1,0:T(8,128)(2,1)S(1)} collective-permute-done((s16[32,2304]{1,0:T(8,128)(2,1)S(1)}, s16[32,2304]{1,0:T(8,128)(2,1)S(1)}, u32[]{:S(2)}, u32[]{:S(2)}) %collective-permute-start.8) | collective-permute-done | bytes 147488 | tf_op jit(solution)/shard_map/ppermute | solution.py:443
  101.3 0.0 collective-permute-done.9.refs_1_
  101.3 0.9 join.1
  102.3 8.2 %all-to-all-start.2 = ((s16[8,16,640]{2,1,0:T(8,128)(2,1)}), s16[8,16,640]{2,1,0:T(8,128)(2,1)S(1)}, u32[]{:S(2)}, u32[]{:S(2)}) async-start(s16[8,16,640]{2,1,0:T(8,128)(2,1)} %join.1), calls=%async_computation.2 | async-start | bytes 327680 | tf_op jit(solution)/shard_map/all_to_all | solution.py:445
  110.4 8.3 %all-to-all-done.2.got_ref = s16[8,16,640]{2,1,0:T(8,128)(2,1)S(1)} async-done(((s16[8,16,640]{2,1,0:T(8,128)(2,1)}), s16[8,16,640]{2,1,0:T(8,128)(2,1)S(1)}, u32[]{:S(2)}, u32[]{:S(2)}) %all-to-all-start.2) | async-done | bytes 163872 | tf_op jit(solution)/shard_map/all_to_all | solution.py:445
  118.7 0.1 zsum.1
  118.9 4.3 %collective-permute-start.11 = (f32[2,2048]{1,0:T(2,128)S(1)}, f32[2,2048]{1,0:T(2,128)S(1)}, u32[]{:S(2)}, u32[]{:S(2)}) collective-permute-start(f32[2,2048]{1,0:T(2,128)S(1)} %constant_dynamic-slice_fusion), channel_id=1, source_target_pairs={{0,1},{1,0},{2,3},{3,2},{4,5},{5,4},{6,7},{7,6},{8,9},{9,8},{10,11... | collective-permute-start | bytes 49160 | tf_op jit(solution)/shard_map/ppermute | solution.py:411
  123.2 0.8 collective-permute-done.11
  124.1 0.6 pad_maximum_fusion
  (4 shorter events, 0.1 us)
Async XLA Ops:
  31.9 21.3 %all-to-all-start.1 = ((bf16[32,8,16,128]{3,2,1,0:T(8,128)(2,1)}), bf16[32,8,16,128]{3,2,1,0:T(8,128)(2,1)S(1)}, u32[]{:S(2)}, u32[]{:S(2)}) async-start(bf16[32,8,16,128]{3,2,1,0:T(8,128)(2,1)} %bitcast.6), calls=%async_computation.1 | async-start | bytes 2097152 | tf_op jit(solution)/shard_map/all_to_all | solution.py:391
  37.7 16.3 %collective-permute-start.2 = (bf16[512,1024]{1,0:T(8,128)(2,1)S(1)}, bf16[512,1024]{1,0:T(8,128)(2,1)S(1)}, u32[]{:S(2)}, u32[]{:S(2)}) collective-permute-start(bf16[512,1024]{1,0:T(8,128)(2,1)S(1)} %halves.1), channel_id=1, source_target_pairs={{0,1},{1,0},{2,3},{3,2},{4,5},{5,4},{6,7},{7,6},{8,9},{9,8},{10,11... | collective-permute-start | bytes 3145736 | tf_op jit(solution)/shard_map/ppermute | solution.py:411
  53.4 2.0 %collective-permute-start = (bf16[16,8,16,128]{3,2,1,0:T(8,128)(2,1)S(1)}, bf16[16,8,16,128]{3,2,1,0:T(8,128)(2,1)S(1)}, u32[]{:S(2)}, u32[]{:S(2)}) collective-permute-start(bf16[16,8,16,128]{3,2,1,0:T(8,128)(2,1)S(1)} %get-tuple-element.46), channel_id=1, source_target_pairs={{0,1},{1,0},{2,3},{3,2},{4,5},{5,4},{6,7},{7,6},{8,9},{9,8},{10,11... | collective-permute-start | bytes 1572872 | tf_op jit(solution)/shard_map/ppermute | solution.py:411
  53.9 2.3 %collective-permute-start.1 = (bf16[16,8,16,128]{3,2,1,0:T(8,128)(2,1)S(1)}, bf16[16,8,16,128]{3,2,1,0:T(8,128)(2,1)S(1)}, u32[]{:S(2)}, u32[]{:S(2)}) collective-permute-start(bf16[16,8,16,128]{3,2,1,0:T(8,128)(2,1)S(1)} %get-tuple-element.45), channel_id=1, source_target_pairs={{0,1},{1,0},{2,3},{3,2},{4,5},{5,4},{6,7},{7,6},{8,9},{9,8},{10,11... | collective-permute-start | bytes 1572872 | tf_op jit(solution)/shard_map/ppermute | solution.py:411
  75.2 12.2 %collective-permute-start.5 = (bf16[512,1024]{1,0:T(8,128)(2,1)S(1)}, bf16[512,1024]{1,0:T(8,128)(2,1)S(1)}, u32[]{:S(2)}, u32[]{:S(2)}) collective-permute-start(bf16[512,1024]{1,0:T(8,128)(2,1)S(1)} %get-tuple-element.30), channel_id=1, source_target_pairs={{0,1},{1,0},{2,3},{3,2},{4,5},{5,4},{6,7},{7,6},{8,9},{9,8},{10,11... | collective-permute-start | bytes 3145736 | tf_op jit(solution)/shard_map/ppermute | solution.py:411
  75.7 9.9 %collective-permute-start.3 = (s16[272,1024]{1,0:T(8,128)(2,1)S(1)}, s16[272,1024]{1,0:T(8,128)(2,1)S(1)}, u32[]{:S(2)}, u32[]{:S(2)}) collective-permute-start(s16[272,1024]{1,0:T(8,128)(2,1)S(1)} %get-tuple-element.27), channel_id=1, source_target_pairs={{0,6},{1,25},{2,4},{3,27},{4,2},{5,29},{6,0},{7,31},{8,14},{9,17},... | collective-permute-start | bytes 1671176 | tf_op jit(solution)/shard_map/ppermute | solution.py:422
  76.2 9.8 %collective-permute-start.6 = (s16[272,1024]{1,0:T(8,128)(2,1)S(1)}, s16[272,1024]{1,0:T(8,128)(2,1)S(1)}, u32[]{:S(2)}, u32[]{:S(2)}) collective-permute-start(s16[272,1024]{1,0:T(8,128)(2,1)S(1)} %get-tuple-element.36), channel_id=1, source_target_pairs={{0,2},{1,9},{2,0},{3,11},{4,6},{5,13},{6,4},{7,15},{8,10},{9,1},{1... | collective-permute-start | bytes 1671176 | tf_op jit(solution)/shard_map/ppermute | solution.py:422
  85.9 6.0 %collective-permute-start.4 = (s16[144,1024]{1,0:T(8,128)(2,1)S(1)}, s16[144,1024]{1,0:T(8,128)(2,1)S(1)}, u32[]{:S(2)}, u32[]{:S(2)}) collective-permute-start(s16[144,1024]{1,0:T(8,128)(2,1)S(1)} %get-tuple-element.28), channel_id=1, source_target_pairs={{0,2},{1,9},{2,0},{3,11},{4,6},{5,13},{6,4},{7,15},{8,10},{9,1},{1... | collective-permute-start | bytes 884744 | tf_op jit(solution)/shard_map/ppermute | solution.py:428
  86.4 7.2 %collective-permute-start.7 = (s16[144,1024]{1,0:T(8,128)(2,1)S(1)}, s16[144,1024]{1,0:T(8,128)(2,1)S(1)}, u32[]{:S(2)}, u32[]{:S(2)}) collective-permute-start(s16[144,1024]{1,0:T(8,128)(2,1)S(1)} %get-tuple-element.38), channel_id=1, source_target_pairs={{0,6},{1,25},{2,4},{3,27},{4,2},{5,29},{6,0},{7,31},{8,14},{9,17},... | collective-permute-start | bytes 884744 | tf_op jit(solution)/shard_map/ppermute | solution.py:428
  93.9 5.7 %collective-permute-start.10 = (s16[32,2304]{1,0:T(8,128)(2,1)S(1)}, s16[32,2304]{1,0:T(8,128)(2,1)S(1)}, u32[]{:S(2)}, u32[]{:S(2)}) collective-permute-start(s16[32,2304]{1,0:T(8,128)(2,1)S(1)} %get-tuple-element.44), channel_id=1, source_target_pairs={{0,16},{1,5},{2,18},{3,7},{4,20},{5,1},{6,22},{7,3},{8,24},{9,13},... | collective-permute-start | bytes 442376 | tf_op jit(solution)/shard_map/ppermute | solution.py:443
  94.3 7.0 %collective-permute-start.8 = (s16[32,2304]{1,0:T(8,128)(2,1)S(1)}, s16[32,2304]{1,0:T(8,128)(2,1)S(1)}, u32[]{:S(2)}, u32[]{:S(2)}) collective-permute-start(s16[32,2304]{1,0:T(8,128)(2,1)S(1)} %get-tuple-element.42), channel_id=1, source_target_pairs={{0,24},{1,7},{2,26},{3,5},{4,28},{5,3},{6,30},{7,1},{8,16},{9,15},... | collective-permute-start | bytes 442376 | tf_op jit(solution)/shard_map/ppermute | solution.py:443
  96.0 5.3 %collective-permute-start.9 = (s16[32,2304]{1,0:T(8,128)(2,1)S(1)}, s16[32,2304]{1,0:T(8,128)(2,1)S(1)}, u32[]{:S(2)}, u32[]{:S(2)}) collective-permute-start(s16[32,2304]{1,0:T(8,128)(2,1)S(1)} %get-tuple-element.43), channel_id=1, source_target_pairs={{0,8},{1,3},{2,10},{3,1},{4,12},{5,7},{6,14},{7,5},{8,0},{9,11},{1... | collective-permute-start | bytes 442376 | tf_op jit(solution)/shard_map/ppermute | solution.py:443
  102.3 16.5 %all-to-all-start.2 = ((s16[8,16,640]{2,1,0:T(8,128)(2,1)}), s16[8,16,640]{2,1,0:T(8,128)(2,1)S(1)}, u32[]{:S(2)}, u32[]{:S(2)}) async-start(s16[8,16,640]{2,1,0:T(8,128)(2,1)} %join.1), calls=%async_computation.2 | async-start | bytes 327680 | tf_op jit(solution)/shard_map/all_to_all | solution.py:445
  118.9 5.2 %collective-permute-start.11 = (f32[2,2048]{1,0:T(2,128)S(1)}, f32[2,2048]{1,0:T(2,128)S(1)}, u32[]{:S(2)}, u32[]{:S(2)}) collective-permute-start(f32[2,2048]{1,0:T(2,128)S(1)} %constant_dynamic-slice_fusion), channel_id=1, source_target_pairs={{0,1},{1,0},{2,3},{3,2},{4,5},{5,4},{6,7},{7,6},{8,9},{9,8},{10,11... | collective-permute-start | bytes 49160 | tf_op jit(solution)/shard_map/ppermute | solution.py:411

commit v3 on v2

--- a/solution.py
+++ b/solution.py
@@ -65,14 +65,16 @@
 
 
 def pick_kernel(spots_ref, store_ref, out_ref):
-    def one(d, carry):
-        spots = [spots_ref[d, k] for k in range(WANT)]
+    batch = 4
+
+    def some(d, carry):
+        spots = [spots_ref[d * batch + i, k] for i in range(batch) for k in range(WANT)]
         tiles = [store_ref[spot >> 3, spot & 7] for spot in spots]
-        for k in range(WANT):
-            out_ref[d * WANT + k] = tiles[k]
+        for i, tile in enumerate(tiles):
+            out_ref[d * batch * WANT + i] = tile
         return carry
 
-    lax.fori_loop(0, out_ref.shape[0] // WANT, one, 0, unroll=8)
+    lax.fori_loop(0, N_DB // batch, some, 0, unroll=2)
 
 
 def encode(x):
@@ -186,31 +188,46 @@
         for p in range(PAIRS)
         for s in range(NC * tokens // STRETCH)
     ]
-    scores, dprob, pbs, ds = [], [], [], []
     k_ref[...] = jnp.dot(f, wk_ref[...], preferred_element_type=jnp.float32).astype(jnp.bfloat16)
     v_ref[...] = jnp.dot(f, wv_ref[...], preferred_element_type=jnp.float32).astype(jnp.bfloat16)
-    for s, keys, cols in items:
-        scores.append(
-            lax.dot_general(k_ref[keys, cols], query(s, cols), NT, preferred_element_type=jnp.float32) * scale
-        )
-        dprob.append(lax.dot_general(v_ref[keys, cols], grad(s, cols), NT, preferred_element_type=jnp.float32))
-    for x, dp in zip(scores, dprob):
-        expo = jnp.exp(x - jnp.max(x, axis=0, keepdims=True))
-        probs = expo * (1.0 / jnp.sum(expo, axis=0, keepdims=True))
+
+    def score(item):
+        s, keys, cols = item
+        scores = lax.dot_general(query(s, cols), k_ref[keys, cols], NT, preferred_element_type=jnp.float32) * scale
+        return scores, lax.dot_general(grad(s, cols), v_ref[keys, cols], NT, preferred_element_type=jnp.float32)
+
+    def soften(x, dp):
+        expo = jnp.exp(x - jnp.max(x, axis=1, keepdims=True))
+        probs = expo * (1.0 / jnp.sum(expo, axis=1, keepdims=True))
         pb = probs.astype(jnp.bfloat16)
-        delta = jnp.sum(pb.astype(jnp.float32) * dp, axis=0, keepdims=True)
-        pbs.append(pb)
-        ds.append((probs * (dp - delta)).astype(jnp.bfloat16))
-    for i, (s, keys, cols) in enumerate(items):
-        dv_ref[keys, cols] = jnp.dot(pbs[i], grad(s, cols), preferred_element_type=jnp.float32).astype(jnp.bfloat16)
-        ctx = lax.dot_general(pbs[i], v_ref[keys, cols], TN, preferred_element_type=jnp.float32)
-        give(0, s, cols.start, ctx)
-    for i, (s, keys, cols) in enumerate(items):
-        dk_ref[keys, cols] = (
-            jnp.dot(ds[i], query(s, cols), preferred_element_type=jnp.float32) * scale
-        ).astype(jnp.bfloat16)
-        dq = lax.dot_general(ds[i], k_ref[keys, cols], TN, preferred_element_type=jnp.float32) * scale
-        give(tokens, s, cols.start, dq)
+        delta = jnp.sum(pb.astype(jnp.float32) * dp, axis=1, keepdims=True)
+        return pb, (probs * (dp - delta)).astype(jnp.bfloat16)
+
+    def value_side(item, pb):
+        s, keys, cols = item
+        give(0, s, cols.start, jnp.dot(pb, v_ref[keys, cols], preferred_element_type=jnp.float32))
+        dv = lax.dot_general(pb, grad(s, cols), TN, preferred_element_type=jnp.float32)
+        dv_ref[keys, cols] = dv.astype(jnp.bfloat16)
+
+    def key_side(item, ds):
+        s, keys, cols = item
+        dk = lax.dot_general(ds, query(s, cols), TN, preferred_element_type=jnp.float32) * scale
+        dk_ref[keys, cols] = dk.astype(jnp.bfloat16)
+        give(tokens, s, cols.start, jnp.dot(ds, k_ref[keys, cols], preferred_element_type=jnp.float32) * scale)
+
+    each = len(items) // PAIRS
+    first, second = items[:each], items[each:]
+    raw_a = [score(item) for item in first]
+    raw_b = [score(item) for item in second]
+    soft_a = [soften(*raw) for raw in raw_a]
+    soft_b = []
+    for i in range(each):
+        value_side(first[i], soft_a[i][0])
+        soft_b.append(soften(*raw_b[i]))
+        key_side(first[i], soft_a[i][1])
+    for i in range(each):
+        value_side(second[i], soft_b[i][0])
+        key_side(second[i], soft_b[i][1])
     dwv = jnp.dot(ft_ref[...], dv_ref[...], preferred_element_type=jnp.float32)
     keepv_ref[:128, :] = dwv[:128]
     keepv_ref[128:, :] = dwv[256:384]

time: 125 us -> 125 us (level)
  no operation moved by 1% of the time
where the time goes in v3:
time: 125 us
  waiting for transfers between devices  44.6 us (36%)
  Pallas kernels  28.8 us (23%)
  blocking collectives  27.3 us (22%)
  starting transfers between devices  22.5 us (18%)
    all_to_all x1, blocking collectives, fetch(): lax.all_to_all(pieces, PLANE, split_axis=0, concat_axis=0, tiled=True)  27.3 us
    pallas_call x1, Pallas kernels, attend(): pl.pallas_call(first_kernel, grid_spec=pltpu.PrefetchScalarGridSpec(num_s...  19.2 us
    all_to_all x1, waiting for transfers between devices, fetch(): lax.all_to_all(picked.reshape(N_DB, WANT, TILE_R, DH), PLANE, split_axis=...  15.1 us
    ppermute x1, waiting for transfers between devices, one(): lax.ppermute(send_v, PLANE, hops(3, 0))  9.31 us
    all_to_all x1, waiting for transfers between devices, body(): got = lax.all_to_all(pieces, 'z', split_axis=0, concat_axis=0, tiled=True)  8.29 us
    all_to_all x1, starting transfers between devices, body(): got = lax.all_to_all(pieces, 'z', split_axis=0, concat_axis=0, tiled=True)  8.19 us
    ppermute x5, starting transfers between devices, body(): swap = lambda v: lax.ppermute(v, 'core', [(0, 1), (1, 0)])  5.84 us
    pallas_call x7, Pallas kernels, local(): pl.pallas_call(kernel, in_specs=smem + [space] * len(args), out_specs=jax...  5.68 us
  transfers between devices with their start and end apart: 14, of which 10 were waited for; matrix products, arithmetic and copies ran while one was open for 0% of the time, Pallas kernels for 3%

profile of v3, /device:TPU:1, one launch (start us, length us, event | category | flops | bytes accessed | tf_op | source)
XLA Modules:
  0.0 124.9 jit_solution(9303973576360009107)
XLA Ops:
  0.6 0.1 pad_add_fusion.coords_ref
  0.7 1.5 %spread.1 = bf16[32,9,16,128]{3,2,1,0:T(8,128)(2,1)S(1)} custom-call(s32[4]{0:T(128)S(1)} %pad_add_fusion.coords_ref, s32[2,4]{1,0:T(2,128)} %bitcast.8, s32[256]{0:T(256)} %home_hbm.1, bf16[8,128,512]{2,1,0:T(8,128)(2,1)} %cache_ref.1), custom_call_target="tpu_custom_call" | custom-call | tf_op jit(solution)/shard_map/spread/pallas_call | solution.py:381
  2.2 27.3 %all_to_all.15.store_ref = bf16[32,9,16,128]{3,2,1,0:T(8,128)(2,1)S(1)} all-to-all(bf16[32,9,16,128]{3,2,1,0:T(8,128)(2,1)S(1)} %spread.1), channel_id=1, replica_groups=mesh['z'=8,'y'=4,'x'=4,'core'=2] {'y','x','core'}, dimensions={0} | all-to-all | bytes 2359296 | tf_op jit(solution)/shard_map/all_to_all | solution.py:397
  29.5 2.4 %pick.1 = bf16[256,16,128]{2,1,0:T(8,128)(2,1)} custom-call(s32[32,8]{1,0:T(8,128)S(1)} %bitcast.7, bf16[32,9,16,128]{3,2,1,0:T(8,128)(2,1)S(1)} %all_to_all.15.store_ref), custom_call_target="tpu_custom_call" | custom-call | tf_op jit(solution)/shard_map/pick/pallas_call | solution.py:399
  31.9 4.0 %all-to-all-start.1 = ((bf16[32,8,16,128]{3,2,1,0:T(8,128)(2,1)}), bf16[32,8,16,128]{3,2,1,0:T(8,128)(2,1)S(1)}, u32[]{:S(2)}, u32[]{:S(2)}) async-start(bf16[32,8,16,128]{3,2,1,0:T(8,128)(2,1)} %bitcast.6), calls=%async_computation.1 | async-start | bytes 2097152 | tf_op jit(solution)/shard_map/all_to_all | solution.py:408
  35.9 1.8 %halves.1 = bf16[512,1024]{1,0:T(8,128)(2,1)S(1)} custom-call(s32[4]{0:T(128)S(1)} %pad_add_fusion.coords_ref, bf16[256,2048]{1,0:T(8,128)(2,1)} %q_ref.3, bf16[256,2048]{1,0:T(8,128)(2,1)} %g_ref.3), custom_call_target="tpu_custom_call" | custom-call | tf_op jit(solution)/shard_map/halves/pallas_call | solution.py:366
  37.7 0.4 collective-permute-start.2
  38.1 15.1 %all-to-all-done.1.r_ref = bf16[32,8,16,128]{3,2,1,0:T(8,128)(2,1)S(1)} async-done(((bf16[32,8,16,128]{3,2,1,0:T(8,128)(2,1)}), bf16[32,8,16,128]{3,2,1,0:T(8,128)(2,1)S(1)}, u32[]{:S(2)}, u32[]{:S(2)}) %all-to-all-start.1) | async-done | bytes 1048608 | tf_op jit(solution)/shard_map/all_to_all | solution.py:408
  53.2 0.2 fusion
  53.4 0.5 collective-permute-start
  53.9 0.1 collective-permute-start.1
  54.0 0.0 collective-permute-done.2.qg_ref
  54.0 1.4 %collective-permute-done.rr0_ref = bf16[16,8,16,128]{3,2,1,0:T(8,128)(2,1)S(1)} collective-permute-done((bf16[16,8,16,128]{3,2,1,0:T(8,128)(2,1)S(1)}, bf16[16,8,16,128]{3,2,1,0:T(8,128)(2,1)S(1)}, u32[]{:S(2)}, u32[]{:S(2)}) %collective-permute-start) | collective-permute-done | bytes 524320 | tf_op jit(solution)/shard_map/ppermute | solution.py:428
  55.4 0.7 collective-permute-done.1.rr1_ref
  56.2 19.2 %attend.1 = (bf16[512,1024]{1,0:T(8,128)(2,1)S(1)}, bf16[512,1024]{1,0:T(8,128)(2,1)S(1)}, f32[256,1024]{1,0:T(8,128)S(1)}, s16[272,1024]{1,0:T(8,128)(2,1)S(1)}...) custom-call(s32[4]{0:T(128)S(1)} %pad_add_fusion.coords_ref, bf16[32,8,16,128]{3,2,1,0:T(8,128)(2,1)S(1)} %all-to-all-done.1.r_ref, ...), custom_call_target="tpu_custom_call" | custom-call | flops 11000000512 | bytes 8388608 | tf_op jit(solution)/shard_map/attend/pallas_call | solution.py:250
  75.4 0.5 collective-permute-start.5
  75.8 0.6 collective-permute-start.3
  76.4 0.0 collective-permute-start.6
  76.4 9.3 %collective-permute-done.3.came_ref = s16[272,1024]{1,0:T(8,128)(2,1)S(1)} collective-permute-done((s16[272,1024]{1,0:T(8,128)(2,1)S(1)}, s16[272,1024]{1,0:T(8,128)(2,1)S(1)}, u32[]{:S(2)}, u32[]{:S(2)}) %collective-permute-start.3) | collective-permute-done | bytes 557088 | tf_op jit(solution)/shard_map/ppermute | solution.py:439
  85.7 0.3 fold.2
  86.0 0.1 collective-permute-start.4
  86.1 0.0 collective-permute-done.6.came_ref
  86.1 0.3 fold.3
  86.5 1.1 collective-permute-start.7
  87.6 0.0 collective-permute-done.5.refs_1_
  87.6 1.9 %place.1 = (bf16[256,2048]{1,0:T(8,128)(2,1)}, bf16[256,2048]{1,0:T(8,128)(2,1)}) custom-call(s32[4]{0:T(128)S(1)} %pad_add_fusion.coords_ref, bf16[512,1024]{1,0:T(8,128)(2,1)S(1)} %get-tuple-element.29.refs_0_, bf16[512,1024]{1,0:T(8,128)(2,1)S(1)} %collective-permute-done.5.refs_1_), custom_call_target="tpu_custom_call" | custom-call | tf_op jit(solution)/shard_map/place/pallas_call | solution.py:366
  89.5 2.5 %collective-permute-done.4.refs_3_ = s16[144,1024]{1,0:T(8,128)(2,1)S(1)} collective-permute-done((s16[144,1024]{1,0:T(8,128)(2,1)S(1)}, s16[144,1024]{1,0:T(8,128)(2,1)S(1)}, u32[]{:S(2)}, u32[]{:S(2)}) %collective-permute-start.4) | collective-permute-done | bytes 294944 | tf_op jit(solution)/shard_map/ppermute | solution.py:445
  92.0 1.7 %collective-permute-done.7.refs_1_ = s16[144,1024]{1,0:T(8,128)(2,1)S(1)} collective-permute-done((s16[144,1024]{1,0:T(8,128)(2,1)S(1)}, s16[144,1024]{1,0:T(8,128)(2,1)S(1)}, u32[]{:S(2)}, u32[]{:S(2)}) %collective-permute-start.7) | collective-permute-done | bytes 294944 | tf_op jit(solution)/shard_map/ppermute | solution.py:445
  93.6 0.3 split.1
  94.0 0.5 collective-permute-start.10
  94.5 1.7 %collective-permute-start.8 = (s16[32,2304]{1,0:T(8,128)(2,1)S(1)}, s16[32,2304]{1,0:T(8,128)(2,1)S(1)}, u32[]{:S(2)}, u32[]{:S(2)}) collective-permute-start(s16[32,2304]{1,0:T(8,128)(2,1)S(1)} %get-tuple-element.42), channel_id=1, source_target_pairs={{0,24},{1,7},{2,26},{3,5},{4,28},{5,3},{6,30},{7,1},{8,16},{9,15},... | collective-permute-start | bytes 442376 | tf_op jit(solution)/shard_map/ppermute | solution.py:460
  96.2 0.6 collective-permute-start.9
  96.7 3.0 %collective-permute-done.10.refs_2_ = s16[32,2304]{1,0:T(8,128)(2,1)S(1)} collective-permute-done((s16[32,2304]{1,0:T(8,128)(2,1)S(1)}, s16[32,2304]{1,0:T(8,128)(2,1)S(1)}, u32[]{:S(2)}, u32[]{:S(2)}) %collective-permute-start.10) | collective-permute-done | bytes 147488 | tf_op jit(solution)/shard_map/ppermute | solution.py:460
  99.7 1.8 %collective-permute-done.8.refs_0_ = s16[32,2304]{1,0:T(8,128)(2,1)S(1)} collective-permute-done((s16[32,2304]{1,0:T(8,128)(2,1)S(1)}, s16[32,2304]{1,0:T(8,128)(2,1)S(1)}, u32[]{:S(2)}, u32[]{:S(2)}) %collective-permute-start.8) | collective-permute-done | bytes 147488 | tf_op jit(solution)/shard_map/ppermute | solution.py:460
  101.5 0.0 collective-permute-done.9.refs_1_
  101.5 0.9 join.1
  102.4 8.2 %all-to-all-start.2 = ((s16[8,16,640]{2,1,0:T(8,128)(2,1)}), s16[8,16,640]{2,1,0:T(8,128)(2,1)S(1)}, u32[]{:S(2)}, u32[]{:S(2)}) async-start(s16[8,16,640]{2,1,0:T(8,128)(2,1)} %join.1), calls=%async_computation.2 | async-start | bytes 327680 | tf_op jit(solution)/shard_map/all_to_all | solution.py:462
  110.6 8.3 %all-to-all-done.2.got_ref = s16[8,16,640]{2,1,0:T(8,128)(2,1)S(1)} async-done(((s16[8,16,640]{2,1,0:T(8,128)(2,1)}), s16[8,16,640]{2,1,0:T(8,128)(2,1)S(1)}, u32[]{:S(2)}, u32[]{:S(2)}) %all-to-all-start.2) | async-done | bytes 163872 | tf_op jit(solution)/shard_map/all_to_all | solution.py:462
  118.9 0.1 zsum.1
  119.0 4.3 %collective-permute-start.11 = (f32[2,2048]{1,0:T(2,128)S(1)}, f32[2,2048]{1,0:T(2,128)S(1)}, u32[]{:S(2)}, u32[]{:S(2)}) collective-permute-start(f32[2,2048]{1,0:T(2,128)S(1)} %constant_dynamic-slice_fusion), channel_id=1, source_target_pairs={{0,1},{1,0},{2,3},{3,2},{4,5},{5,4},{6,7},{7,6},{8,9},{9,8},{10,11... | collective-permute-start | bytes 49160 | tf_op jit(solution)/shard_map/ppermute | solution.py:428
  123.4 0.8 collective-permute-done.11
  124.2 0.6 pad_maximum_fusion
  (4 shorter events, 0.0 us)
Async XLA Ops:
  31.9 21.3 %all-to-all-start.1 = ((bf16[32,8,16,128]{3,2,1,0:T(8,128)(2,1)}), bf16[32,8,16,128]{3,2,1,0:T(8,128)(2,1)S(1)}, u32[]{:S(2)}, u32[]{:S(2)}) async-start(bf16[32,8,16,128]{3,2,1,0:T(8,128)(2,1)} %bitcast.6), calls=%async_computation.1 | async-start | bytes 2097152 | tf_op jit(solution)/shard_map/all_to_all | solution.py:408
  37.7 16.3 %collective-permute-start.2 = (bf16[512,1024]{1,0:T(8,128)(2,1)S(1)}, bf16[512,1024]{1,0:T(8,128)(2,1)S(1)}, u32[]{:S(2)}, u32[]{:S(2)}) collective-permute-start(bf16[512,1024]{1,0:T(8,128)(2,1)S(1)} %halves.1), channel_id=1, source_target_pairs={{0,1},{1,0},{2,3},{3,2},{4,5},{5,4},{6,7},{7,6},{8,9},{9,8},{10,11... | collective-permute-start | bytes 3145736 | tf_op jit(solution)/shard_map/ppermute | solution.py:428
  53.4 2.0 %collective-permute-start = (bf16[16,8,16,128]{3,2,1,0:T(8,128)(2,1)S(1)}, bf16[16,8,16,128]{3,2,1,0:T(8,128)(2,1)S(1)}, u32[]{:S(2)}, u32[]{:S(2)}) collective-permute-start(bf16[16,8,16,128]{3,2,1,0:T(8,128)(2,1)S(1)} %get-tuple-element.46), channel_id=1, source_target_pairs={{0,1},{1,0},{2,3},{3,2},{4,5},{5,4},{6,7},{7,6},{8,9},{9,8},{10,11... | collective-permute-start | bytes 1572872 | tf_op jit(solution)/shard_map/ppermute | solution.py:428
  53.9 2.3 %collective-permute-start.1 = (bf16[16,8,16,128]{3,2,1,0:T(8,128)(2,1)S(1)}, bf16[16,8,16,128]{3,2,1,0:T(8,128)(2,1)S(1)}, u32[]{:S(2)}, u32[]{:S(2)}) collective-permute-start(bf16[16,8,16,128]{3,2,1,0:T(8,128)(2,1)S(1)} %get-tuple-element.45), channel_id=1, source_target_pairs={{0,1},{1,0},{2,3},{3,2},{4,5},{5,4},{6,7},{7,6},{8,9},{9,8},{10,11... | collective-permute-start | bytes 1572872 | tf_op jit(solution)/shard_map/ppermute | solution.py:428
  75.4 12.2 %collective-permute-start.5 = (bf16[512,1024]{1,0:T(8,128)(2,1)S(1)}, bf16[512,1024]{1,0:T(8,128)(2,1)S(1)}, u32[]{:S(2)}, u32[]{:S(2)}) collective-permute-start(bf16[512,1024]{1,0:T(8,128)(2,1)S(1)} %get-tuple-element.30), channel_id=1, source_target_pairs={{0,1},{1,0},{2,3},{3,2},{4,5},{5,4},{6,7},{7,6},{8,9},{9,8},{10,11... | collective-permute-start | bytes 3145736 | tf_op jit(solution)/shard_map/ppermute | solution.py:428
  75.8 9.9 %collective-permute-start.3 = (s16[272,1024]{1,0:T(8,128)(2,1)S(1)}, s16[272,1024]{1,0:T(8,128)(2,1)S(1)}, u32[]{:S(2)}, u32[]{:S(2)}) collective-permute-start(s16[272,1024]{1,0:T(8,128)(2,1)S(1)} %get-tuple-element.27), channel_id=1, source_target_pairs={{0,6},{1,25},{2,4},{3,27},{4,2},{5,29},{6,0},{7,31},{8,14},{9,17},... | collective-permute-start | bytes 1671176 | tf_op jit(solution)/shard_map/ppermute | solution.py:439
  76.4 9.8 %collective-permute-start.6 = (s16[272,1024]{1,0:T(8,128)(2,1)S(1)}, s16[272,1024]{1,0:T(8,128)(2,1)S(1)}, u32[]{:S(2)}, u32[]{:S(2)}) collective-permute-start(s16[272,1024]{1,0:T(8,128)(2,1)S(1)} %get-tuple-element.36), channel_id=1, source_target_pairs={{0,2},{1,9},{2,0},{3,11},{4,6},{5,13},{6,4},{7,15},{8,10},{9,1},{1... | collective-permute-start | bytes 1671176 | tf_op jit(solution)/shard_map/ppermute | solution.py:439
  86.0 6.0 %collective-permute-start.4 = (s16[144,1024]{1,0:T(8,128)(2,1)S(1)}, s16[144,1024]{1,0:T(8,128)(2,1)S(1)}, u32[]{:S(2)}, u32[]{:S(2)}) collective-permute-start(s16[144,1024]{1,0:T(8,128)(2,1)S(1)} %get-tuple-element.28), channel_id=1, source_target_pairs={{0,2},{1,9},{2,0},{3,11},{4,6},{5,13},{6,4},{7,15},{8,10},{9,1},{1... | collective-permute-start | bytes 884744 | tf_op jit(solution)/shard_map/ppermute | solution.py:445
  86.5 7.2 %collective-permute-start.7 = (s16[144,1024]{1,0:T(8,128)(2,1)S(1)}, s16[144,1024]{1,0:T(8,128)(2,1)S(1)}, u32[]{:S(2)}, u32[]{:S(2)}) collective-permute-start(s16[144,1024]{1,0:T(8,128)(2,1)S(1)} %get-tuple-element.38), channel_id=1, source_target_pairs={{0,6},{1,25},{2,4},{3,27},{4,2},{5,29},{6,0},{7,31},{8,14},{9,17},... | collective-permute-start | bytes 884744 | tf_op jit(solution)/shard_map/ppermute | solution.py:445
  94.0 5.7 %collective-permute-start.10 = (s16[32,2304]{1,0:T(8,128)(2,1)S(1)}, s16[32,2304]{1,0:T(8,128)(2,1)S(1)}, u32[]{:S(2)}, u32[]{:S(2)}) collective-permute-start(s16[32,2304]{1,0:T(8,128)(2,1)S(1)} %get-tuple-element.44), channel_id=1, source_target_pairs={{0,16},{1,5},{2,18},{3,7},{4,20},{5,1},{6,22},{7,3},{8,24},{9,13},... | collective-permute-start | bytes 442376 | tf_op jit(solution)/shard_map/ppermute | solution.py:460
  94.5 7.0 %collective-permute-start.8 = (s16[32,2304]{1,0:T(8,128)(2,1)S(1)}, s16[32,2304]{1,0:T(8,128)(2,1)S(1)}, u32[]{:S(2)}, u32[]{:S(2)}) collective-permute-start(s16[32,2304]{1,0:T(8,128)(2,1)S(1)} %get-tuple-element.42), channel_id=1, source_target_pairs={{0,24},{1,7},{2,26},{3,5},{4,28},{5,3},{6,30},{7,1},{8,16},{9,15},... | collective-permute-start | bytes 442376 | tf_op jit(solution)/shard_map/ppermute | solution.py:460
  96.2 5.3 %collective-permute-start.9 = (s16[32,2304]{1,0:T(8,128)(2,1)S(1)}, s16[32,2304]{1,0:T(8,128)(2,1)S(1)}, u32[]{:S(2)}, u32[]{:S(2)}) collective-permute-start(s16[32,2304]{1,0:T(8,128)(2,1)S(1)} %get-tuple-element.43), channel_id=1, source_target_pairs={{0,8},{1,3},{2,10},{3,1},{4,12},{5,7},{6,14},{7,5},{8,0},{9,11},{1... | collective-permute-start | bytes 442376 | tf_op jit(solution)/shard_map/ppermute | solution.py:460
  102.4 16.5 %all-to-all-start.2 = ((s16[8,16,640]{2,1,0:T(8,128)(2,1)}), s16[8,16,640]{2,1,0:T(8,128)(2,1)S(1)}, u32[]{:S(2)}, u32[]{:S(2)}) async-start(s16[8,16,640]{2,1,0:T(8,128)(2,1)} %join.1), calls=%async_computation.2 | async-start | bytes 327680 | tf_op jit(solution)/shard_map/all_to_all | solution.py:462
  119.0 5.2 %collective-permute-start.11 = (f32[2,2048]{1,0:T(2,128)S(1)}, f32[2,2048]{1,0:T(2,128)S(1)}, u32[]{:S(2)}, u32[]{:S(2)}) collective-permute-start(f32[2,2048]{1,0:T(2,128)S(1)} %constant_dynamic-slice_fusion), channel_id=1, source_target_pairs={{0,1},{1,0},{2,3},{3,2},{4,5},{5,4},{6,7},{7,6},{8,9},{9,8},{10,11... | collective-permute-start | bytes 49160 | tf_op jit(solution)/shard_map/ppermute | solution.py:428

commit v4 on v2

--- a/solution.py
+++ b/solution.py
@@ -67,7 +67,7 @@
 def pick_kernel(spots_ref, store_ref, out_ref):
     def one(d, carry):
         spots = [spots_ref[d, k] for k in range(WANT)]
-        tiles = [store_ref[spot >> 3, spot & 7] for spot in spots]
+        tiles = [store_ref[spot] for spot in spots]
         for k in range(WANT):
             out_ref[d * WANT + k] = tiles[k]
         return carry
@@ -124,43 +124,59 @@
     return jnp.where(new == place, 1.0, 0.0).astype(jnp.bfloat16)
 
 
-def lay_rows(coords_ref, r_ref, rr_refs, f_ref, ft_ref):
-    half = RB * FB // 2
-    for side in range(NC):
-        for rb in range(RB):
-            for fb in range(FB):
-                m = rb * FB + fb
-                ref, at = (r_ref, m) if side == 0 else (rr_refs[m // half], m % half)
-                for w in range(WANT):
-                    f_ref[side * WANT + w, rb, :, fb * DH : (fb + 1) * DH] = ref[at, w]
-    f = f_ref[...].reshape(NC * WANT * ROWS, FEAT)
+def lay_rows(coords_ref, refs, f_ref, ft_ref):
+    each = RB * FB // len(refs)
+    for rb in range(RB):
+        for fb in range(FB):
+            m = rb * FB + fb
+            for w in range(WANT):
+                f_ref[w, rb, :, fb * DH : (fb + 1) * DH] = refs[m // each][m % each, w]
+    f = f_ref[...].reshape(WANT * ROWS, FEAT)
     ft_ref[...] = lax.dot_general(row_order(coords_ref), f, NT, preferred_element_type=jnp.float32).astype(
         jnp.bfloat16
     )
 
 
-def first_kernel(coords_ref, r_ref, rr0_ref, rr1_ref, q_ref, g_ref, qg_ref, wk_ref, wv_ref, *refs):
-    outs, f_ref, ft_ref, scratch = refs[:6], refs[6], refs[7], refs[8:]
-
-    @pl.when(pl.program_id(0) == 0)
-    def _():
-        lay_rows(coords_ref, r_ref, (rr0_ref, rr1_ref), f_ref, ft_ref)
-
-    attend_kernel(coords_ref, f_ref, ft_ref, q_ref, g_ref, qg_ref, wk_ref, wv_ref, *outs, *scratch)
+def project(f_ref, wk_ref, wv_ref, k_ref, v_ref):
+    f = f_ref[...].reshape(WANT * ROWS, FEAT)
+    k_ref[...] = jnp.dot(f, wk_ref[...], preferred_element_type=jnp.float32).astype(jnp.bfloat16)
+    v_ref[...] = jnp.dot(f, wv_ref[...], preferred_element_type=jnp.float32).astype(jnp.bfloat16)
+
+
+def own_kernel(coords_ref, r_ref, f_ref, ft_ref):
+    lay_rows(coords_ref, (r_ref,), f_ref, ft_ref)
 
 
 def attend_kernel(
-    coords_ref, f_ref, ft_ref, q_ref, g_ref, qg_ref, wk_ref, wv_ref,
+    coords_ref, rr0_ref, rr1_ref, f0_ref, ft0_ref, q_ref, g_ref, qg_ref, wk_ref, wv_ref,
     own_ref, oth_ref, keepk_ref, sendk_ref, keepv_ref, sendv_ref,
-    k_ref, v_ref, dk_ref, dv_ref,
+    f1_ref, ft1_ref, k0_ref, v0_ref, k1_ref, v1_ref, dk_ref, dv_ref,
 ):
     scale = DH ** (-0.5)
     tokens = q_ref.shape[0]
-    every = NC * WANT * ROWS
+    near = WANT * ROWS
+
+    @pl.when(pl.program_id(0) == 0)
+    def _():
+        lay_rows(coords_ref, (rr0_ref, rr1_ref), f1_ref, ft1_ref)
+
+    project(f0_ref, wk_ref, wv_ref, k0_ref, v0_ref)
+    project(f1_ref, wk_ref, wv_ref, k1_ref, v1_ref)
+
+    def held(refs, keys, cols):
+        ref, at = (refs[0], keys.start) if keys.start < near else (refs[1], keys.start - near)
+        return ref[at : at + KEYS, cols]
+
+    keyed = functools.partial(held, (k0_ref, k1_ref))
+    valued = functools.partial(held, (v0_ref, v1_ref))
+
+    def weight(rows, grad_ref):
+        return jnp.dot(ft0_ref[rows, :], grad_ref[:near, :], preferred_element_type=jnp.float32) + jnp.dot(
+            ft1_ref[rows, :], grad_ref[near:, :], preferred_element_type=jnp.float32
+        )
+
     left = lax.broadcasted_iota(jnp.int32, (STRETCH, PAIR), 1) < DH
     zero = jnp.zeros((STRETCH, PAIR), jnp.bfloat16)
-    f = f_ref[...].reshape(every, FEAT)
-
     def both(t):
         return jnp.concatenate([jnp.where(left, t, zero), jnp.where(left, zero, t)], axis=0)
 
@@ -187,13 +203,11 @@
         for s in range(NC * tokens // STRETCH)
     ]
     scores, dprob, pbs, ds = [], [], [], []
-    k_ref[...] = jnp.dot(f, wk_ref[...], preferred_element_type=jnp.float32).astype(jnp.bfloat16)
-    v_ref[...] = jnp.dot(f, wv_ref[...], preferred_element_type=jnp.float32).astype(jnp.bfloat16)
     for s, keys, cols in items:
         scores.append(
-            lax.dot_general(k_ref[keys, cols], query(s, cols), NT, preferred_element_type=jnp.float32) * scale
+            lax.dot_general(keyed(keys, cols), query(s, cols), NT, preferred_element_type=jnp.float32) * scale
         )
-        dprob.append(lax.dot_general(v_ref[keys, cols], grad(s, cols), NT, preferred_element_type=jnp.float32))
+        dprob.append(lax.dot_general(valued(keys, cols), grad(s, cols), NT, preferred_element_type=jnp.float32))
     for x, dp in zip(scores, dprob):
         expo = jnp.exp(x - jnp.max(x, axis=0, keepdims=True))
         probs = expo * (1.0 / jnp.sum(expo, axis=0, keepdims=True))
@@ -203,49 +217,57 @@
         ds.append((probs * (dp - delta)).astype(jnp.bfloat16))
     for i, (s, keys, cols) in enumerate(items):
         dv_ref[keys, cols] = jnp.dot(pbs[i], grad(s, cols), preferred_element_type=jnp.float32).astype(jnp.bfloat16)
-        ctx = lax.dot_general(pbs[i], v_ref[keys, cols], TN, preferred_element_type=jnp.float32)
+        ctx = lax.dot_general(pbs[i], valued(keys, cols), TN, preferred_element_type=jnp.float32)
         give(0, s, cols.start, ctx)
     for i, (s, keys, cols) in enumerate(items):
         dk_ref[keys, cols] = (
             jnp.dot(ds[i], query(s, cols), preferred_element_type=jnp.float32) * scale
         ).astype(jnp.bfloat16)
-        dq = lax.dot_general(ds[i], k_ref[keys, cols], TN, preferred_element_type=jnp.float32) * scale
+        dq = lax.dot_general(ds[i], keyed(keys, cols), TN, preferred_element_type=jnp.float32) * scale
         give(tokens, s, cols.start, dq)
-    dwv = jnp.dot(ft_ref[...], dv_ref[...], preferred_element_type=jnp.float32)
+    dwv = weight(slice(None), dv_ref)
     keepv_ref[:128, :] = dwv[:128]
     keepv_ref[128:, :] = dwv[256:384]
     put(sendv_ref, jnp.concatenate([dwv[128:256], dwv[384:]], axis=0))
-    put(sendk_ref, jnp.dot(ft_ref[256:, :], dk_ref[...], preferred_element_type=jnp.float32))
-    keepk_ref[...] = jnp.dot(ft_ref[:256, :], dk_ref[...], preferred_element_type=jnp.float32)
-
-
-def attend(coords, rows, queries, grad_out, oth, kv_weight):
+    put(sendk_ref, weight(slice(256, None), dk_ref))
+    keepk_ref[...] = weight(slice(0, 256), dk_ref)
+
+
+def weight_specs(width):
+    steps = width // WIDE // NC
+    return [
+        pl.BlockSpec((FEAT, WIDE), lambda h, at, skip=skip: (0, skip + at[3] * steps + h)) for skip in (0, NC * steps)
+    ]
+
+
+def attend(coords, rows, f0, ft0, queries, grad_out, oth, kv_weight):
     tokens, width = queries.shape
     steps = width // WIDE // NC
     half = FEAT // 2
-    every = NC * WANT * ROWS
+    near = WANT * ROWS
     queries, grad_out, kv_weight = (
         pltpu.with_memory_space_constraint(a, pltpu.HBM) for a in (queries, grad_out, kv_weight)
     )
-    mine = lambda rows, at0: pl.BlockSpec((rows, WIDE), lambda h, at: (0, at0 + at[3] * steps + h))
+    vmem = pl.BlockSpec(memory_space=pltpu.VMEM)
+    mine = pl.BlockSpec((tokens, WIDE), lambda h, at: (0, at[3] * steps + h))
     col = lambda rows: pl.BlockSpec((rows, WIDE), lambda h, at: (0, h))
     shape = lambda rows, dtype: jax.ShapeDtypeStruct((rows, width // NC), dtype)
     return pl.pallas_call(
-        first_kernel,
+        attend_kernel,
         grid_spec=pltpu.PrefetchScalarGridSpec(
             num_scalar_prefetch=1,
             grid=(steps,),
-            in_specs=[pl.BlockSpec(memory_space=pltpu.VMEM)] * 3
-            + [mine(tokens, 0), mine(tokens, 0), col(2 * tokens), mine(FEAT, 0), mine(FEAT, NC * steps)],
+            in_specs=[vmem] * 4 + [mine, mine, col(2 * tokens)] + weight_specs(width),
             out_specs=[
                 col(2 * tokens), col(2 * tokens),
                 col(half), col(half + TILE_R), col(half), col(half + TILE_R),
             ],
             scratch_shapes=[
-                pltpu.VMEM((NC * WANT, RB, TILE_R, FEAT), jnp.bfloat16),
-                pltpu.VMEM((FEAT, every), jnp.bfloat16),
+                pltpu.VMEM((WANT, RB, TILE_R, FEAT), jnp.bfloat16),
+                pltpu.VMEM((FEAT, near), jnp.bfloat16),
             ]
-            + [pltpu.VMEM((every, WIDE), jnp.bfloat16)] * 4,
+            + [pltpu.VMEM((near, WIDE), jnp.bfloat16)] * 4
+            + [pltpu.VMEM((NC * near, WIDE), jnp.bfloat16)] * 2,
         ),
         out_shape=[
             shape(2 * tokens, jnp.bfloat16), shape(2 * tokens, jnp.bfloat16),
@@ -253,9 +275,9 @@
             shape(half, jnp.float32), shape(half + TILE_R, jnp.int16),
         ],
         compiler_params=pltpu.CompilerParams(vmem_limit_bytes=36 * 2**20),
-        cost_estimate=pl.CostEstimate(flops=11 * 10**9, bytes_accessed=8 * 2**20, transcendentals=10**6),
+        cost_estimate=pl.CostEstimate(flops=9 * 10**9, bytes_accessed=8 * 2**20, transcendentals=10**6),
         name="attend",
-    )(coords, *rows, queries, grad_out, oth, kv_weight, kv_weight)
+    )(coords, *rows, f0, ft0, queries, grad_out, oth, kv_weight, kv_weight)
 
 
 def fold_kernel(kept_ref, came_ref, keep_ref, send_ref):
@@ -379,6 +401,8 @@
     )
     store = lax.all_to_all(pieces, PLANE, split_axis=0, concat_axis=0, tiled=True)
     spots = store[:, ents, 0, :WANT].astype(jnp.int32)
+    spots = spots + (spots >> 3)
+    store = store.reshape(N_DB * (ents + 1), TILE_R, DH)
     picked = pl.pallas_call(
         pick_kernel,
         in_specs=[smem, vmem],
@@ -429,7 +453,11 @@
         return out
 
     args = (queries, grad_out, oth, kv_weight)
-    own, other, *grads = attend(coords, (answer, swap(answer[:16]), swap(answer[16:])), *args)
+    rows = (swap(answer[:16]), swap(answer[16:]))
+    laid = [pltpu.VMEM((WANT, RB, TILE_R, FEAT), jnp.bfloat16), pltpu.VMEM((FEAT, WANT * ROWS), jnp.bfloat16)]
+    laid = local(own_kernel, "own_side", laid, answer, coords=coords)
+    rows, laid = tie((rows, laid))
+    own, other, *grads = attend(coords, rows, *laid, *args)
     sums = one(*grads)
     other = swap(other)
     sums = two(*sums)

time: 125 us -> 124 us (level)
  waiting for transfers between devices: 44.6 us -> 43.3 us
    pallas_call x7 -> x8, Pallas kernels: 5.68 us -> 7.01 us  [local(): pl.pallas_call(kernel, in_specs=smem + [space] * len(args), out_specs=jax...]
    ppermute x5, waiting for transfers between devices: 3.01 us -> 1.68 us  [body(): swap = lambda v: lax.ppermute(v, 'core', [(0, 1), (1, 0)])]
  transfers between devices with their start and end apart: 14 -> 14, of which waited for: 10 -> 10; matrix products, arithmetic and copies ran while one was open for 0% -> 0% of each run, Pallas kernels for 3% -> 5%
where the time goes in v4:
time: 124 us
  waiting for transfers between devices  43.3 us (35%)
  Pallas kernels  29.2 us (24%)
  blocking collectives  27.3 us (22%)
  starting transfers between devices  22.5 us (18%)
    all_to_all x1, blocking collectives, fetch(): lax.all_to_all(pieces, PLANE, split_axis=0, concat_axis=0, tiled=True)  27.3 us
    pallas_call x1, Pallas kernels, attend(): pl.pallas_call(attend_kernel, grid_spec=pltpu.PrefetchScalarGridSpec(num_...  18.6 us
    all_to_all x1, waiting for transfers between devices, fetch(): lax.all_to_all(picked.reshape(N_DB, WANT, TILE_R, DH), PLANE, split_axis=...  15.1 us
    ppermute x1, waiting for transfers between devices, one(): lax.ppermute(send_v, PLANE, hops(3, 0))  9.34 us
    all_to_all x1, waiting for transfers between devices, body(): got = lax.all_to_all(pieces, 'z', split_axis=0, concat_axis=0, tiled=True)  8.29 us
    all_to_all x1, starting transfers between devices, body(): got = lax.all_to_all(pieces, 'z', split_axis=0, concat_axis=0, tiled=True)  8.17 us
    pallas_call x8, Pallas kernels, local(): pl.pallas_call(kernel, in_specs=smem + [space] * len(args), out_specs=jax...  7.01 us
    ppermute x5, starting transfers between devices, body(): swap = lambda v: lax.ppermute(v, 'core', [(0, 1), (1, 0)])  5.86 us
  transfers between devices with their start and end apart: 14, of which 10 were waited for; matrix products, arithmetic and copies ran while one was open for 0% of the time, Pallas kernels for 5%

profile of v4, /device:TPU:1, one launch (start us, length us, event | category | flops | bytes accessed | tf_op | source)
XLA Modules:
  0.0 123.9 jit_solution(5682464167321940251)
XLA Ops:
  0.6 0.1 pad_add_fusion.coords_ref
  0.7 1.5 %spread.1 = bf16[32,9,16,128]{3,2,1,0:T(8,128)(2,1)S(1)} custom-call(s32[4]{0:T(128)S(1)} %pad_add_fusion.coords_ref, s32[2,4]{1,0:T(2,128)} %bitcast.13, s32[256]{0:T(256)} %home_hbm.1, bf16[8,128,512]{2,1,0:T(8,128)(2,1)} %cache_ref.1), custom_call_target="tpu_custom_call" | custom-call | tf_op jit(solution)/shard_map/spread/pallas_call | solution.py:386
  2.2 27.3 %all_to_all.15 = bf16[32,9,16,128]{3,2,1,0:T(8,128)(2,1)S(1)} all-to-all(bf16[32,9,16,128]{3,2,1,0:T(8,128)(2,1)S(1)} %spread.1), channel_id=1, replica_groups=mesh['z'=8,'y'=4,'x'=4,'core'=2] {'y','x','core'}, dimensions={0} | all-to-all | bytes 2359296 | tf_op jit(solution)/shard_map/all_to_all | solution.py:402
  29.5 2.1 %pick.1 = bf16[256,16,128]{2,1,0:T(8,128)(2,1)} custom-call(s32[32,8]{1,0:T(8,128)S(1)} %shift-right-arithmetic_add_fusion.spots_ref, bf16[288,16,128]{2,1,0:T(8,128)(2,1)S(1)} %bitcast.12), custom_call_target="tpu_custom_call" | custom-call | tf_op jit(solution)/shard_map/pick/pallas_call | solution.py:406
  31.6 4.0 %all-to-all-start.1 = ((bf16[32,8,16,128]{3,2,1,0:T(8,128)(2,1)}), bf16[32,8,16,128]{3,2,1,0:T(8,128)(2,1)S(1)}, u32[]{:S(2)}, u32[]{:S(2)}) async-start(bf16[32,8,16,128]{3,2,1,0:T(8,128)(2,1)} %bitcast.8), calls=%async_computation.1 | async-start | bytes 2097152 | tf_op jit(solution)/shard_map/all_to_all | solution.py:415
  35.6 1.8 %halves.1 = bf16[512,1024]{1,0:T(8,128)(2,1)S(1)} custom-call(s32[4]{0:T(128)S(1)} %pad_add_fusion.coords_ref, bf16[256,2048]{1,0:T(8,128)(2,1)} %q_ref.3, bf16[256,2048]{1,0:T(8,128)(2,1)} %g_ref.3), custom_call_target="tpu_custom_call" | custom-call | tf_op jit(solution)/shard_map/halves/pallas_call | solution.py:371
  37.4 0.4 collective-permute-start.2
  37.8 15.1 %all-to-all-done.1.r_ref = bf16[32,8,16,128]{3,2,1,0:T(8,128)(2,1)S(1)} async-done(((bf16[32,8,16,128]{3,2,1,0:T(8,128)(2,1)}), bf16[32,8,16,128]{3,2,1,0:T(8,128)(2,1)S(1)}, u32[]{:S(2)}, u32[]{:S(2)}) %all-to-all-start.1) | async-done | bytes 1048608 | tf_op jit(solution)/shard_map/all_to_all | solution.py:415
  52.9 0.2 fusion
  53.1 0.5 collective-permute-start
  53.5 0.1 collective-permute-start.1
  53.7 1.3 %own_side.1 = (bf16[8,8,16,512]{3,2,1,0:T(8,128)(2,1)S(1)}, bf16[512,1024]{1,0:T(8,128)(2,1)S(1)}) custom-call(s32[4]{0:T(128)S(1)} %pad_add_fusion.coords_ref, bf16[32,8,16,128]{3,2,1,0:T(8,128)(2,1)S(1)} %all-to-all-done.1.r_ref), custom_call_target="tpu_custom_call" | custom-call | tf_op jit(solution)/shard_map/own_side/pallas_call | solution.py:371
  55.0 0.1 collective-permute-done.rr0_ref
  55.1 0.7 collective-permute-done.1.rr1_ref
  55.8 0.0 collective-permute-done.2.qg_ref
  55.8 18.6 %attend.1 = (bf16[512,1024]{1,0:T(8,128)(2,1)S(1)}, bf16[512,1024]{1,0:T(8,128)(2,1)S(1)}, f32[256,1024]{1,0:T(8,128)S(1)}, s16[272,1024]{1,0:T(8,128)(2,1)S(1)}...) custom-call(s32[4]{0:T(128)S(1)} %pad_add_fusion.coords_ref, ...), custom_call_target="tpu_custom_call" | custom-call | flops 8999999488 | bytes 8388608 | tf_op jit(solution)/shard_map/attend/pallas_call | solution.py:255
  74.4 0.5 collective-permute-start.5
  74.9 0.5 collective-permute-start.3
  75.4 0.0 collective-permute-start.6
  75.4 9.3 %collective-permute-done.3.came_ref = s16[272,1024]{1,0:T(8,128)(2,1)S(1)} collective-permute-done((s16[272,1024]{1,0:T(8,128)(2,1)S(1)}, s16[272,1024]{1,0:T(8,128)(2,1)S(1)}, u32[]{:S(2)}, u32[]{:S(2)}) %collective-permute-start.3) | collective-permute-done | bytes 557088 | tf_op jit(solution)/shard_map/ppermute | solution.py:446
  84.8 0.3 fold.2
  85.1 0.1 collective-permute-start.4
  85.2 0.0 collective-permute-done.6.came_ref
  85.2 0.3 fold.3
  85.6 1.1 collective-permute-start.7
  86.7 0.0 collective-permute-done.5.refs_1_
  86.7 1.9 %place.1 = (bf16[256,2048]{1,0:T(8,128)(2,1)}, bf16[256,2048]{1,0:T(8,128)(2,1)}) custom-call(s32[4]{0:T(128)S(1)} %pad_add_fusion.coords_ref, bf16[512,1024]{1,0:T(8,128)(2,1)S(1)} %get-tuple-element.41.refs_0_, bf16[512,1024]{1,0:T(8,128)(2,1)S(1)} %collective-permute-done.5.refs_1_), custom_call_target="tpu_custom_call" | custom-call | tf_op jit(solution)/shard_map/place/pallas_call | solution.py:371
  88.6 2.5 %collective-permute-done.4.refs_3_ = s16[144,1024]{1,0:T(8,128)(2,1)S(1)} collective-permute-done((s16[144,1024]{1,0:T(8,128)(2,1)S(1)}, s16[144,1024]{1,0:T(8,128)(2,1)S(1)}, u32[]{:S(2)}, u32[]{:S(2)}) %collective-permute-start.4) | collective-permute-done | bytes 294944 | tf_op jit(solution)/shard_map/ppermute | solution.py:452
  91.1 1.7 %collective-permute-done.7.refs_1_ = s16[144,1024]{1,0:T(8,128)(2,1)S(1)} collective-permute-done((s16[144,1024]{1,0:T(8,128)(2,1)S(1)}, s16[144,1024]{1,0:T(8,128)(2,1)S(1)}, u32[]{:S(2)}, u32[]{:S(2)}) %collective-permute-start.7) | collective-permute-done | bytes 294944 | tf_op jit(solution)/shard_map/ppermute | solution.py:452
  92.7 0.3 split.1
  93.1 0.5 collective-permute-start.10
  93.5 1.7 %collective-permute-start.8 = (s16[32,2304]{1,0:T(8,128)(2,1)S(1)}, s16[32,2304]{1,0:T(8,128)(2,1)S(1)}, u32[]{:S(2)}, u32[]{:S(2)}) collective-permute-start(s16[32,2304]{1,0:T(8,128)(2,1)S(1)} %get-tuple-element.54), channel_id=1, source_target_pairs={{0,24},{1,7},{2,26},{3,5},{4,28},{5,3},{6,30},{7,1},{8,16},{9,15},... | collective-permute-start | bytes 442376 | tf_op jit(solution)/shard_map/ppermute | solution.py:471
  95.2 0.6 collective-permute-start.9
  95.8 3.0 %collective-permute-done.10.refs_2_ = s16[32,2304]{1,0:T(8,128)(2,1)S(1)} collective-permute-done((s16[32,2304]{1,0:T(8,128)(2,1)S(1)}, s16[32,2304]{1,0:T(8,128)(2,1)S(1)}, u32[]{:S(2)}, u32[]{:S(2)}) %collective-permute-start.10) | collective-permute-done | bytes 147488 | tf_op jit(solution)/shard_map/ppermute | solution.py:471
  98.8 1.8 %collective-permute-done.8.refs_0_ = s16[32,2304]{1,0:T(8,128)(2,1)S(1)} collective-permute-done((s16[32,2304]{1,0:T(8,128)(2,1)S(1)}, s16[32,2304]{1,0:T(8,128)(2,1)S(1)}, u32[]{:S(2)}, u32[]{:S(2)}) %collective-permute-start.8) | collective-permute-done | bytes 147488 | tf_op jit(solution)/shard_map/ppermute | solution.py:471
  100.5 0.0 collective-permute-done.9.refs_1_
  100.5 0.9 join.1
  101.5 8.2 %all-to-all-start.2 = ((s16[8,16,640]{2,1,0:T(8,128)(2,1)}), s16[8,16,640]{2,1,0:T(8,128)(2,1)S(1)}, u32[]{:S(2)}, u32[]{:S(2)}) async-start(s16[8,16,640]{2,1,0:T(8,128)(2,1)} %join.1), calls=%async_computation.2 | async-start | bytes 327680 | tf_op jit(solution)/shard_map/all_to_all | solution.py:473
  109.6 8.3 %all-to-all-done.2.got_ref = s16[8,16,640]{2,1,0:T(8,128)(2,1)S(1)} async-done(((s16[8,16,640]{2,1,0:T(8,128)(2,1)}), s16[8,16,640]{2,1,0:T(8,128)(2,1)S(1)}, u32[]{:S(2)}, u32[]{:S(2)}) %all-to-all-start.2) | async-done | bytes 163872 | tf_op jit(solution)/shard_map/all_to_all | solution.py:473
  117.9 0.1 zsum.1
  118.1 4.3 %collective-permute-start.11 = (f32[2,2048]{1,0:T(2,128)S(1)}, f32[2,2048]{1,0:T(2,128)S(1)}, u32[]{:S(2)}, u32[]{:S(2)}) collective-permute-start(f32[2,2048]{1,0:T(2,128)S(1)} %constant_dynamic-slice_fusion), channel_id=1, source_target_pairs={{0,1},{1,0},{2,3},{3,2},{4,5},{5,4},{6,7},{7,6},{8,9},{9,8},{10,11... | collective-permute-start | bytes 49160 | tf_op jit(solution)/shard_map/ppermute | solution.py:435
  122.4 0.8 collective-permute-done.11
  123.3 0.6 pad_maximum_fusion
  (5 shorter events, 0.1 us)
Async XLA Ops:
  31.6 21.3 %all-to-all-start.1 = ((bf16[32,8,16,128]{3,2,1,0:T(8,128)(2,1)}), bf16[32,8,16,128]{3,2,1,0:T(8,128)(2,1)S(1)}, u32[]{:S(2)}, u32[]{:S(2)}) async-start(bf16[32,8,16,128]{3,2,1,0:T(8,128)(2,1)} %bitcast.8), calls=%async_computation.1 | async-start | bytes 2097152 | tf_op jit(solution)/shard_map/all_to_all | solution.py:415
  37.4 18.5 %collective-permute-start.2 = (bf16[512,1024]{1,0:T(8,128)(2,1)S(1)}, bf16[512,1024]{1,0:T(8,128)(2,1)S(1)}, u32[]{:S(2)}, u32[]{:S(2)}) collective-permute-start(bf16[512,1024]{1,0:T(8,128)(2,1)S(1)} %halves.1), channel_id=1, source_target_pairs={{0,1},{1,0},{2,3},{3,2},{4,5},{5,4},{6,7},{7,6},{8,9},{9,8},{10,11... | collective-permute-start | bytes 3145736 | tf_op jit(solution)/shard_map/ppermute | solution.py:435
  53.1 2.0 %collective-permute-start = (bf16[16,8,16,128]{3,2,1,0:T(8,128)(2,1)S(1)}, bf16[16,8,16,128]{3,2,1,0:T(8,128)(2,1)S(1)}, u32[]{:S(2)}, u32[]{:S(2)}) collective-permute-start(bf16[16,8,16,128]{3,2,1,0:T(8,128)(2,1)S(1)} %get-tuple-element.58), channel_id=1, source_target_pairs={{0,1},{1,0},{2,3},{3,2},{4,5},{5,4},{6,7},{7,6},{8,9},{9,8},{10,11... | collective-permute-start | bytes 1572872 | tf_op jit(solution)/shard_map/ppermute | solution.py:435
  53.5 2.3 %collective-permute-start.1 = (bf16[16,8,16,128]{3,2,1,0:T(8,128)(2,1)S(1)}, bf16[16,8,16,128]{3,2,1,0:T(8,128)(2,1)S(1)}, u32[]{:S(2)}, u32[]{:S(2)}) collective-permute-start(bf16[16,8,16,128]{3,2,1,0:T(8,128)(2,1)S(1)} %get-tuple-element.57), channel_id=1, source_target_pairs={{0,1},{1,0},{2,3},{3,2},{4,5},{5,4},{6,7},{7,6},{8,9},{9,8},{10,11... | collective-permute-start | bytes 1572872 | tf_op jit(solution)/shard_map/ppermute | solution.py:435
  74.4 12.3 %collective-permute-start.5 = (bf16[512,1024]{1,0:T(8,128)(2,1)S(1)}, bf16[512,1024]{1,0:T(8,128)(2,1)S(1)}, u32[]{:S(2)}, u32[]{:S(2)}) collective-permute-start(bf16[512,1024]{1,0:T(8,128)(2,1)S(1)} %get-tuple-element.42), channel_id=1, source_target_pairs={{0,1},{1,0},{2,3},{3,2},{4,5},{5,4},{6,7},{7,6},{8,9},{9,8},{10,11... | collective-permute-start | bytes 3145736 | tf_op jit(solution)/shard_map/ppermute | solution.py:435
  74.9 9.9 %collective-permute-start.3 = (s16[272,1024]{1,0:T(8,128)(2,1)S(1)}, s16[272,1024]{1,0:T(8,128)(2,1)S(1)}, u32[]{:S(2)}, u32[]{:S(2)}) collective-permute-start(s16[272,1024]{1,0:T(8,128)(2,1)S(1)} %get-tuple-element.39), channel_id=1, source_target_pairs={{0,6},{1,25},{2,4},{3,27},{4,2},{5,29},{6,0},{7,31},{8,14},{9,17},... | collective-permute-start | bytes 1671176 | tf_op jit(solution)/shard_map/ppermute | solution.py:446
  75.4 9.8 %collective-permute-start.6 = (s16[272,1024]{1,0:T(8,128)(2,1)S(1)}, s16[272,1024]{1,0:T(8,128)(2,1)S(1)}, u32[]{:S(2)}, u32[]{:S(2)}) collective-permute-start(s16[272,1024]{1,0:T(8,128)(2,1)S(1)} %get-tuple-element.48), channel_id=1, source_target_pairs={{0,2},{1,9},{2,0},{3,11},{4,6},{5,13},{6,4},{7,15},{8,10},{9,1},{1... | collective-permute-start | bytes 1671176 | tf_op jit(solution)/shard_map/ppermute | solution.py:446
  85.1 6.0 %collective-permute-start.4 = (s16[144,1024]{1,0:T(8,128)(2,1)S(1)}, s16[144,1024]{1,0:T(8,128)(2,1)S(1)}, u32[]{:S(2)}, u32[]{:S(2)}) collective-permute-start(s16[144,1024]{1,0:T(8,128)(2,1)S(1)} %get-tuple-element.40), channel_id=1, source_target_pairs={{0,2},{1,9},{2,0},{3,11},{4,6},{5,13},{6,4},{7,15},{8,10},{9,1},{1... | collective-permute-start | bytes 884744 | tf_op jit(solution)/shard_map/ppermute | solution.py:452
  85.6 7.2 %collective-permute-start.7 = (s16[144,1024]{1,0:T(8,128)(2,1)S(1)}, s16[144,1024]{1,0:T(8,128)(2,1)S(1)}, u32[]{:S(2)}, u32[]{:S(2)}) collective-permute-start(s16[144,1024]{1,0:T(8,128)(2,1)S(1)} %get-tuple-element.50), channel_id=1, source_target_pairs={{0,6},{1,25},{2,4},{3,27},{4,2},{5,29},{6,0},{7,31},{8,14},{9,17},... | collective-permute-start | bytes 884744 | tf_op jit(solution)/shard_map/ppermute | solution.py:452
  93.1 5.7 %collective-permute-start.10 = (s16[32,2304]{1,0:T(8,128)(2,1)S(1)}, s16[32,2304]{1,0:T(8,128)(2,1)S(1)}, u32[]{:S(2)}, u32[]{:S(2)}) collective-permute-start(s16[32,2304]{1,0:T(8,128)(2,1)S(1)} %get-tuple-element.56), channel_id=1, source_target_pairs={{0,16},{1,5},{2,18},{3,7},{4,20},{5,1},{6,22},{7,3},{8,24},{9,13},... | collective-permute-start | bytes 442376 | tf_op jit(solution)/shard_map/ppermute | solution.py:471
  93.5 7.0 %collective-permute-start.8 = (s16[32,2304]{1,0:T(8,128)(2,1)S(1)}, s16[32,2304]{1,0:T(8,128)(2,1)S(1)}, u32[]{:S(2)}, u32[]{:S(2)}) collective-permute-start(s16[32,2304]{1,0:T(8,128)(2,1)S(1)} %get-tuple-element.54), channel_id=1, source_target_pairs={{0,24},{1,7},{2,26},{3,5},{4,28},{5,3},{6,30},{7,1},{8,16},{9,15},... | collective-permute-start | bytes 442376 | tf_op jit(solution)/shard_map/ppermute | solution.py:471
  95.2 5.3 %collective-permute-start.9 = (s16[32,2304]{1,0:T(8,128)(2,1)S(1)}, s16[32,2304]{1,0:T(8,128)(2,1)S(1)}, u32[]{:S(2)}, u32[]{:S(2)}) collective-permute-start(s16[32,2304]{1,0:T(8,128)(2,1)S(1)} %get-tuple-element.55), channel_id=1, source_target_pairs={{0,8},{1,3},{2,10},{3,1},{4,12},{5,7},{6,14},{7,5},{8,0},{9,11},{1... | collective-permute-start | bytes 442376 | tf_op jit(solution)/shard_map/ppermute | solution.py:471
  101.5 16.5 %all-to-all-start.2 = ((s16[8,16,640]{2,1,0:T(8,128)(2,1)}), s16[8,16,640]{2,1,0:T(8,128)(2,1)S(1)}, u32[]{:S(2)}, u32[]{:S(2)}) async-start(s16[8,16,640]{2,1,0:T(8,128)(2,1)} %join.1), calls=%async_computation.2 | async-start | bytes 327680 | tf_op jit(solution)/shard_map/all_to_all | solution.py:473
  118.1 5.2 %collective-permute-start.11 = (f32[2,2048]{1,0:T(2,128)S(1)}, f32[2,2048]{1,0:T(2,128)S(1)}, u32[]{:S(2)}, u32[]{:S(2)}) collective-permute-start(f32[2,2048]{1,0:T(2,128)S(1)} %constant_dynamic-slice_fusion), channel_id=1, source_target_pairs={{0,1},{1,0},{2,3},{3,2},{4,5},{5,4},{6,7},{7,6},{8,9},{9,8},{10,11... | collective-permute-start | bytes 49160 | tf_op jit(solution)/shard_map/ppermute | solution.py:435

commit v5 on v4

--- a/solution.py
+++ b/solution.py
@@ -319,15 +319,29 @@
         refs[-1][z, :, :wide], refs[-1][z, :, wide:] = encode_rows(mine)
 
 
-def z_kernel(got_ref, out_ref):
+def z_kernel(coords_ref, got_ref, mine_ref, away_ref):
     wide = got_ref.shape[2] - DH
     total = None
     for z in range(NZ):
         piece = decode_rows(got_ref[z, :, :wide], got_ref[z, :, wide:])
         total = piece if z == 0 else total + piece
-    rows = out_ref.shape[0]
+    first = coords_ref[3] == 0
     for q in range(4):
-        out_ref[:, q * wide : (q + 1) * wide] = total[q * rows : (q + 1) * rows]
+        cols = slice(q * wide, (q + 1) * wide)
+        low, high = total[4 * q : 4 * q + 2], total[4 * q + 2 : 4 * q + 4]
+        mine_ref[:, cols] = jnp.where(first, low, high)
+        away_ref[:, cols] = jnp.where(first, high, low)
+
+
+def last_kernel(coords_ref, mine_ref, came_ref, out_ref):
+    first = coords_ref[3] == 0
+    width = mine_ref.shape[1] // 2
+    low = jnp.where(first, mine_ref[...], came_ref[...])
+    high = jnp.where(first, came_ref[...], mine_ref[...])
+    for kv in range(2):
+        for c, half in enumerate((low, high)):
+            at = (kv * NC + c) * width
+            out_ref[:, at : at + width] = half[:, kv * width : (kv + 1) * width]
 
 
 def copy_all(copies):
@@ -471,14 +485,8 @@
     came = [lax.ppermute(v, PLANE, hops(mask, 1)) for v, mask in zip(sent, RING[1:])]
     pieces = local(join_kernel, "join", shape((NZ, 4 * part // NZ, width // 4 + DH), jnp.int16), kept, *came)
     got = lax.all_to_all(pieces, "z", split_axis=0, concat_axis=0, tiled=True)
-    total = local(z_kernel, "zsum", shape((2 * NC, width), jnp.float32), got)
-    core = lax.axis_index("core")
-    mine = lax.dynamic_slice(total, (2 * core, 0), (2, width))
-    came = swap(lax.dynamic_slice(total, (2 - 2 * core, 0), (2, width)))
-    low, high = jnp.where(core == 0, mine, came), jnp.where(core == 0, came, mine)
-    weight_grad = jnp.concatenate(
-        [low[:, : width // 2], high[:, : width // 2], low[:, width // 2 :], high[:, width // 2 :]], axis=1
-    )
+    mine, away = local(z_kernel, "zsum", [shape((2, width), jnp.float32)] * 2, got, coords=coords)
+    weight_grad = local(last_kernel, "last", shape((2, NC * width), jnp.float32), mine, swap(away), coords=coords)
     return (*outs, weight_grad)
 
 

time: 124 us -> 126 us (1.016)
  blocking collectives: 27.3 us -> 43.6 us
  waiting for transfers between devices: 43.3 us -> 34.3 us
  starting transfers between devices: 22.5 us -> 16 us
    all_to_all x0 -> x1, blocking collectives: none -> 16.4 us  [body(): got = lax.all_to_all(pieces, 'z', split_axis=0, concat_axis=0, tiled=True)]
    all_to_all x1 -> x0, waiting for transfers between devices: 8.29 us -> none  [body(): got = lax.all_to_all(pieces, 'z', split_axis=0, concat_axis=0, tiled=True)]
    all_to_all x1 -> x0, starting transfers between devices: 8.17 us -> none  [body(): got = lax.all_to_all(pieces, 'z', split_axis=0, concat_axis=0, tiled=True)]
    pallas_call x8 -> x9, Pallas kernels: 7.01 us -> 8.06 us  [local(): pl.pallas_call(kernel, in_specs=smem + [space] * len(args), out_specs=jax...]
  transfers between devices with their start and end apart: 14 -> 13, of which waited for: 10 -> 9; matrix products, arithmetic and copies ran while one was open for 0% -> 0% of each run, Pallas kernels for 5% -> 4%
where the time goes in v5:
time: 126 us; the launch traced here: 125 us
  blocking collectives  43.6 us (35%)
  waiting for transfers between devices  34.3 us (27%)
  Pallas kernels  30.2 us (24%)
  starting transfers between devices  16 us (13%)
    all_to_all x1, blocking collectives, fetch(): lax.all_to_all(pieces, PLANE, split_axis=0, concat_axis=0, tiled=True)  27.3 us
    pallas_call x1, Pallas kernels, attend(): pl.pallas_call(attend_kernel, grid_spec=pltpu.PrefetchScalarGridSpec(num_...  18.6 us
    all_to_all x1, blocking collectives, body(): got = lax.all_to_all(pieces, 'z', split_axis=0, concat_axis=0, tiled=True)  16.4 us
    all_to_all x1, waiting for transfers between devices, fetch(): lax.all_to_all(picked.reshape(N_DB, WANT, TILE_R, DH), PLANE, split_axis=...  15.1 us
    ppermute x1, waiting for transfers between devices, one(): lax.ppermute(send_v, PLANE, hops(3, 0))  9.31 us
    pallas_call x9, Pallas kernels, local(): pl.pallas_call(kernel, in_specs=smem + [space] * len(args), out_specs=jax...  8.06 us
    ppermute x5, starting transfers between devices, body(): swap = lambda v: lax.ppermute(v, 'core', [(0, 1), (1, 0)])  6.31 us
    ppermute x2, waiting for transfers between devices, two(): out += [kept, lax.ppermute(sent, PLANE, hops(mask, 0))]  4.16 us
  transfers between devices with their start and end apart: 13, of which 9 were waited for; matrix products, arithmetic and copies ran while one was open for 0% of the time, Pallas kernels for 4%

profile of v5, /device:TPU:1, one launch (start us, length us, event | category | flops | bytes accessed | tf_op | source)
XLA Modules:
  0.0 125.3 jit_solution(453049071209960593)
XLA Ops:
  0.6 0.1 pad_add_fusion.coords_ref
  0.7 1.5 %spread.1 = bf16[32,9,16,128]{3,2,1,0:T(8,128)(2,1)S(1)} custom-call(s32[4]{0:T(128)S(1)} %pad_add_fusion.coords_ref, s32[2,4]{1,0:T(2,128)} %bitcast.13, s32[256]{0:T(256)} %home_hbm.1, bf16[8,128,512]{2,1,0:T(8,128)(2,1)} %cache_ref.1), custom_call_target="tpu_custom_call" | custom-call | tf_op jit(solution)/shard_map/spread/pallas_call | solution.py:400
  2.2 27.3 %all_to_all.15 = bf16[32,9,16,128]{3,2,1,0:T(8,128)(2,1)S(1)} all-to-all(bf16[32,9,16,128]{3,2,1,0:T(8,128)(2,1)S(1)} %spread.1), channel_id=1, replica_groups=mesh['z'=8,'y'=4,'x'=4,'core'=2] {'y','x','core'}, dimensions={0} | all-to-all | bytes 2359296 | tf_op jit(solution)/shard_map/all_to_all | solution.py:416
  29.5 2.1 %pick.1 = bf16[256,16,128]{2,1,0:T(8,128)(2,1)} custom-call(s32[32,8]{1,0:T(8,128)S(1)} %shift-right-arithmetic_add_fusion.spots_ref, bf16[288,16,128]{2,1,0:T(8,128)(2,1)S(1)} %bitcast.12), custom_call_target="tpu_custom_call" | custom-call | tf_op jit(solution)/shard_map/pick/pallas_call | solution.py:420
  31.6 4.0 %all-to-all-start.1 = ((bf16[32,8,16,128]{3,2,1,0:T(8,128)(2,1)}), bf16[32,8,16,128]{3,2,1,0:T(8,128)(2,1)S(1)}, u32[]{:S(2)}, u32[]{:S(2)}) async-start(bf16[32,8,16,128]{3,2,1,0:T(8,128)(2,1)} %bitcast.8), calls=%async_computation.1 | async-start | bytes 2097152 | tf_op jit(solution)/shard_map/all_to_all | solution.py:429
  35.6 1.8 %halves.1 = bf16[512,1024]{1,0:T(8,128)(2,1)S(1)} custom-call(s32[4]{0:T(128)S(1)} %pad_add_fusion.coords_ref, bf16[256,2048]{1,0:T(8,128)(2,1)} %q_ref.3, bf16[256,2048]{1,0:T(8,128)(2,1)} %g_ref.3), custom_call_target="tpu_custom_call" | custom-call | tf_op jit(solution)/shard_map/halves/pallas_call | solution.py:385
  37.4 0.4 collective-permute-start.2
  37.8 15.1 %all-to-all-done.1.r_ref = bf16[32,8,16,128]{3,2,1,0:T(8,128)(2,1)S(1)} async-done(((bf16[32,8,16,128]{3,2,1,0:T(8,128)(2,1)}), bf16[32,8,16,128]{3,2,1,0:T(8,128)(2,1)S(1)}, u32[]{:S(2)}, u32[]{:S(2)}) %all-to-all-start.1) | async-done | bytes 1048608 | tf_op jit(solution)/shard_map/all_to_all | solution.py:429
  52.9 0.2 fusion
  53.1 0.5 collective-permute-start.1
  53.5 0.1 collective-permute-start
  53.7 1.3 %own_side.1 = (bf16[8,8,16,512]{3,2,1,0:T(8,128)(2,1)S(1)}, bf16[512,1024]{1,0:T(8,128)(2,1)S(1)}) custom-call(s32[4]{0:T(128)S(1)} %pad_add_fusion.coords_ref, bf16[32,8,16,128]{3,2,1,0:T(8,128)(2,1)S(1)} %all-to-all-done.1.r_ref), custom_call_target="tpu_custom_call" | custom-call | tf_op jit(solution)/shard_map/own_side/pallas_call | solution.py:385
  55.0 0.1 collective-permute-done.1.rr1_ref
  55.1 0.7 collective-permute-done.rr0_ref
  55.8 0.0 collective-permute-done.2.qg_ref
  55.8 18.6 %attend.1 = (bf16[512,1024]{1,0:T(8,128)(2,1)S(1)}, bf16[512,1024]{1,0:T(8,128)(2,1)S(1)}, f32[256,1024]{1,0:T(8,128)S(1)}, s16[272,1024]{1,0:T(8,128)(2,1)S(1)}...) custom-call(s32[4]{0:T(128)S(1)} %pad_add_fusion.coords_ref, ...), custom_call_target="tpu_custom_call" | custom-call | flops 8999999488 | bytes 8388608 | tf_op jit(solution)/shard_map/attend/pallas_call | solution.py:255
  74.4 0.4 collective-permute-start.5
  74.9 0.6 collective-permute-start.3
  75.4 0.0 collective-permute-start.6
  75.4 9.3 %collective-permute-done.3.came_ref = s16[272,1024]{1,0:T(8,128)(2,1)S(1)} collective-permute-done((s16[272,1024]{1,0:T(8,128)(2,1)S(1)}, s16[272,1024]{1,0:T(8,128)(2,1)S(1)}, u32[]{:S(2)}, u32[]{:S(2)}) %collective-permute-start.3) | collective-permute-done | bytes 557088 | tf_op jit(solution)/shard_map/ppermute | solution.py:460
  84.8 0.3 fold.2
  85.1 0.1 collective-permute-start.4
  85.2 0.0 collective-permute-done.6.came_ref
  85.2 0.3 fold.3
  85.5 1.1 collective-permute-start.7
  86.7 0.0 collective-permute-done.5.refs_1_
  86.7 1.9 %place.1 = (bf16[256,2048]{1,0:T(8,128)(2,1)}, bf16[256,2048]{1,0:T(8,128)(2,1)}) custom-call(s32[4]{0:T(128)S(1)} %pad_add_fusion.coords_ref, bf16[512,1024]{1,0:T(8,128)(2,1)S(1)} %get-tuple-element.43.refs_0_, bf16[512,1024]{1,0:T(8,128)(2,1)S(1)} %collective-permute-done.5.refs_1_), custom_call_target="tpu_custom_call" | custom-call | tf_op jit(solution)/shard_map/place/pallas_call | solution.py:385
  88.6 2.5 %collective-permute-done.4.refs_3_ = s16[144,1024]{1,0:T(8,128)(2,1)S(1)} collective-permute-done((s16[144,1024]{1,0:T(8,128)(2,1)S(1)}, s16[144,1024]{1,0:T(8,128)(2,1)S(1)}, u32[]{:S(2)}, u32[]{:S(2)}) %collective-permute-start.4) | collective-permute-done | bytes 294944 | tf_op jit(solution)/shard_map/ppermute | solution.py:466
  91.1 1.7 %collective-permute-done.7.refs_1_ = s16[144,1024]{1,0:T(8,128)(2,1)S(1)} collective-permute-done((s16[144,1024]{1,0:T(8,128)(2,1)S(1)}, s16[144,1024]{1,0:T(8,128)(2,1)S(1)}, u32[]{:S(2)}, u32[]{:S(2)}) %collective-permute-start.7) | collective-permute-done | bytes 294944 | tf_op jit(solution)/shard_map/ppermute | solution.py:466
  92.7 0.3 split.1
  93.1 1.3 %collective-permute-start.8 = (s16[32,2304]{1,0:T(8,128)(2,1)S(1)}, s16[32,2304]{1,0:T(8,128)(2,1)S(1)}, u32[]{:S(2)}, u32[]{:S(2)}) collective-permute-start(s16[32,2304]{1,0:T(8,128)(2,1)S(1)} %get-tuple-element.56), channel_id=1, source_target_pairs={{0,24},{1,7},{2,26},{3,5},{4,28},{5,3},{6,30},{7,1},{8,16},{9,15},... | collective-permute-start | bytes 442376 | tf_op jit(solution)/shard_map/ppermute | solution.py:485
  94.3 0.0 collective-permute-start.9
  94.3 2.7 %collective-permute-start.10 = (s16[32,2304]{1,0:T(8,128)(2,1)S(1)}, s16[32,2304]{1,0:T(8,128)(2,1)S(1)}, u32[]{:S(2)}, u32[]{:S(2)}) collective-permute-start(s16[32,2304]{1,0:T(8,128)(2,1)S(1)} %get-tuple-element.58), channel_id=1, source_target_pairs={{0,16},{1,5},{2,18},{3,7},{4,20},{5,1},{6,22},{7,3},{8,24},{9,13},... | collective-permute-start | bytes 442376 | tf_op jit(solution)/shard_map/ppermute | solution.py:485
  97.0 1.3 %collective-permute-done.8.refs_0_ = s16[32,2304]{1,0:T(8,128)(2,1)S(1)} collective-permute-done((s16[32,2304]{1,0:T(8,128)(2,1)S(1)}, s16[32,2304]{1,0:T(8,128)(2,1)S(1)}, u32[]{:S(2)}, u32[]{:S(2)}) %collective-permute-start.8) | collective-permute-done | bytes 147488 | tf_op jit(solution)/shard_map/ppermute | solution.py:485
  98.3 0.0 collective-permute-done.9.refs_1_
  98.3 2.8 %collective-permute-done.10.refs_2_ = s16[32,2304]{1,0:T(8,128)(2,1)S(1)} collective-permute-done((s16[32,2304]{1,0:T(8,128)(2,1)S(1)}, s16[32,2304]{1,0:T(8,128)(2,1)S(1)}, u32[]{:S(2)}, u32[]{:S(2)}) %collective-permute-start.10) | collective-permute-done | bytes 147488 | tf_op jit(solution)/shard_map/ppermute | solution.py:485
  101.1 0.3 join.1
  101.4 16.4 %all_to_all.16.got_ref = s16[8,16,640]{2,1,0:T(8,128)(2,1)S(1)} all-to-all(s16[8,16,640]{2,1,0:T(8,128)(2,1)S(1)} %join.1), channel_id=1, replica_groups=mesh['z'=8,'y'=4,'x'=4,'core'=2] {'z'}, dimensions={0} | all-to-all | bytes 327680 | tf_op jit(solution)/shard_map/all_to_all | solution.py:487
  117.8 0.6 zsum.1
  118.4 4.8 %collective-permute-start.11 = (f32[2,2048]{1,0:T(2,128)S(1)}, f32[2,2048]{1,0:T(2,128)S(1)}, u32[]{:S(2)}, u32[]{:S(2)}) collective-permute-start(f32[2,2048]{1,0:T(2,128)S(1)} %get-tuple-element.60), channel_id=1, source_target_pairs={{0,1},{1,0},{2,3},{3,2},{4,5},{5,4},{6,7},{7,6},{8,9},{9,8},{10,11... | collective-permute-start | bytes 49160 | tf_op jit(solution)/shard_map/ppermute | solution.py:449
  123.3 0.8 collective-permute-done.11.came_ref
  124.1 1.2 last.1
  (2 shorter events, 0.0 us)
Async XLA Ops:
  31.6 21.3 %all-to-all-start.1 = ((bf16[32,8,16,128]{3,2,1,0:T(8,128)(2,1)}), bf16[32,8,16,128]{3,2,1,0:T(8,128)(2,1)S(1)}, u32[]{:S(2)}, u32[]{:S(2)}) async-start(bf16[32,8,16,128]{3,2,1,0:T(8,128)(2,1)} %bitcast.8), calls=%async_computation.1 | async-start | bytes 2097152 | tf_op jit(solution)/shard_map/all_to_all | solution.py:429
  37.4 18.5 %collective-permute-start.2 = (bf16[512,1024]{1,0:T(8,128)(2,1)S(1)}, bf16[512,1024]{1,0:T(8,128)(2,1)S(1)}, u32[]{:S(2)}, u32[]{:S(2)}) collective-permute-start(bf16[512,1024]{1,0:T(8,128)(2,1)S(1)} %halves.1), channel_id=1, source_target_pairs={{0,1},{1,0},{2,3},{3,2},{4,5},{5,4},{6,7},{7,6},{8,9},{9,8},{10,11... | collective-permute-start | bytes 3145736 | tf_op jit(solution)/shard_map/ppermute | solution.py:449
  53.1 2.0 %collective-permute-start.1 = (bf16[16,8,16,128]{3,2,1,0:T(8,128)(2,1)S(1)}, bf16[16,8,16,128]{3,2,1,0:T(8,128)(2,1)S(1)}, u32[]{:S(2)}, u32[]{:S(2)}) collective-permute-start(bf16[16,8,16,128]{3,2,1,0:T(8,128)(2,1)S(1)} %get-tuple-element.61), channel_id=1, source_target_pairs={{0,1},{1,0},{2,3},{3,2},{4,5},{5,4},{6,7},{7,6},{8,9},{9,8},{10,11... | collective-permute-start | bytes 1572872 | tf_op jit(solution)/shard_map/ppermute | solution.py:449
  53.5 2.3 %collective-permute-start = (bf16[16,8,16,128]{3,2,1,0:T(8,128)(2,1)S(1)}, bf16[16,8,16,128]{3,2,1,0:T(8,128)(2,1)S(1)}, u32[]{:S(2)}, u32[]{:S(2)}) collective-permute-start(bf16[16,8,16,128]{3,2,1,0:T(8,128)(2,1)S(1)} %get-tuple-element.62), channel_id=1, source_target_pairs={{0,1},{1,0},{2,3},{3,2},{4,5},{5,4},{6,7},{7,6},{8,9},{9,8},{10,11... | collective-permute-start | bytes 1572872 | tf_op jit(solution)/shard_map/ppermute | solution.py:449
  74.4 12.2 %collective-permute-start.5 = (bf16[512,1024]{1,0:T(8,128)(2,1)S(1)}, bf16[512,1024]{1,0:T(8,128)(2,1)S(1)}, u32[]{:S(2)}, u32[]{:S(2)}) collective-permute-start(bf16[512,1024]{1,0:T(8,128)(2,1)S(1)} %get-tuple-element.44), channel_id=1, source_target_pairs={{0,1},{1,0},{2,3},{3,2},{4,5},{5,4},{6,7},{7,6},{8,9},{9,8},{10,11... | collective-permute-start | bytes 3145736 | tf_op jit(solution)/shard_map/ppermute | solution.py:449
  74.9 9.9 %collective-permute-start.3 = (s16[272,1024]{1,0:T(8,128)(2,1)S(1)}, s16[272,1024]{1,0:T(8,128)(2,1)S(1)}, u32[]{:S(2)}, u32[]{:S(2)}) collective-permute-start(s16[272,1024]{1,0:T(8,128)(2,1)S(1)} %get-tuple-element.41), channel_id=1, source_target_pairs={{0,6},{1,25},{2,4},{3,27},{4,2},{5,29},{6,0},{7,31},{8,14},{9,17},... | collective-permute-start | bytes 1671176 | tf_op jit(solution)/shard_map/ppermute | solution.py:460
  75.4 9.8 %collective-permute-start.6 = (s16[272,1024]{1,0:T(8,128)(2,1)S(1)}, s16[272,1024]{1,0:T(8,128)(2,1)S(1)}, u32[]{:S(2)}, u32[]{:S(2)}) collective-permute-start(s16[272,1024]{1,0:T(8,128)(2,1)S(1)} %get-tuple-element.50), channel_id=1, source_target_pairs={{0,2},{1,9},{2,0},{3,11},{4,6},{5,13},{6,4},{7,15},{8,10},{9,1},{1... | collective-permute-start | bytes 1671176 | tf_op jit(solution)/shard_map/ppermute | solution.py:460
  85.1 6.0 %collective-permute-start.4 = (s16[144,1024]{1,0:T(8,128)(2,1)S(1)}, s16[144,1024]{1,0:T(8,128)(2,1)S(1)}, u32[]{:S(2)}, u32[]{:S(2)}) collective-permute-start(s16[144,1024]{1,0:T(8,128)(2,1)S(1)} %get-tuple-element.42), channel_id=1, source_target_pairs={{0,2},{1,9},{2,0},{3,11},{4,6},{5,13},{6,4},{7,15},{8,10},{9,1},{1... | collective-permute-start | bytes 884744 | tf_op jit(solution)/shard_map/ppermute | solution.py:466
  85.5 7.2 %collective-permute-start.7 = (s16[144,1024]{1,0:T(8,128)(2,1)S(1)}, s16[144,1024]{1,0:T(8,128)(2,1)S(1)}, u32[]{:S(2)}, u32[]{:S(2)}) collective-permute-start(s16[144,1024]{1,0:T(8,128)(2,1)S(1)} %get-tuple-element.52), channel_id=1, source_target_pairs={{0,6},{1,25},{2,4},{3,27},{4,2},{5,29},{6,0},{7,31},{8,14},{9,17},... | collective-permute-start | bytes 884744 | tf_op jit(solution)/shard_map/ppermute | solution.py:466
  93.1 5.3 %collective-permute-start.8 = (s16[32,2304]{1,0:T(8,128)(2,1)S(1)}, s16[32,2304]{1,0:T(8,128)(2,1)S(1)}, u32[]{:S(2)}, u32[]{:S(2)}) collective-permute-start(s16[32,2304]{1,0:T(8,128)(2,1)S(1)} %get-tuple-element.56), channel_id=1, source_target_pairs={{0,24},{1,7},{2,26},{3,5},{4,28},{5,3},{6,30},{7,1},{8,16},{9,15},... | collective-permute-start | bytes 442376 | tf_op jit(solution)/shard_map/ppermute | solution.py:485
  94.3 4.0 %collective-permute-start.9 = (s16[32,2304]{1,0:T(8,128)(2,1)S(1)}, s16[32,2304]{1,0:T(8,128)(2,1)S(1)}, u32[]{:S(2)}, u32[]{:S(2)}) collective-permute-start(s16[32,2304]{1,0:T(8,128)(2,1)S(1)} %get-tuple-element.57), channel_id=1, source_target_pairs={{0,8},{1,3},{2,10},{3,1},{4,12},{5,7},{6,14},{7,5},{8,0},{9,11},{1... | collective-permute-start | bytes 442376 | tf_op jit(solution)/shard_map/ppermute | solution.py:485
  94.3 6.8 %collective-permute-start.10 = (s16[32,2304]{1,0:T(8,128)(2,1)S(1)}, s16[32,2304]{1,0:T(8,128)(2,1)S(1)}, u32[]{:S(2)}, u32[]{:S(2)}) collective-permute-start(s16[32,2304]{1,0:T(8,128)(2,1)S(1)} %get-tuple-element.58), channel_id=1, source_target_pairs={{0,16},{1,5},{2,18},{3,7},{4,20},{5,1},{6,22},{7,3},{8,24},{9,13},... | collective-permute-start | bytes 442376 | tf_op jit(solution)/shard_map/ppermute | solution.py:485
  118.4 5.7 %collective-permute-start.11 = (f32[2,2048]{1,0:T(2,128)S(1)}, f32[2,2048]{1,0:T(2,128)S(1)}, u32[]{:S(2)}, u32[]{:S(2)}) collective-permute-start(f32[2,2048]{1,0:T(2,128)S(1)} %get-tuple-element.60), channel_id=1, source_target_pairs={{0,1},{1,0},{2,3},{3,2},{4,5},{5,4},{6,7},{7,6},{8,9},{9,8},{10,11... | collective-permute-start | bytes 49160 | tf_op jit(solution)/shard_map/ppermute | solution.py:449
